TPU v7x, 32 devices: a whole 2x2x4 slice. The times are simulated.
32 devices in a mesh: dp: 16 (over z, y, core), mp: 2 (over x).
Axes of the slice: x: 2, y: 2, z: 4, core: 2. Of those that a mesh axis runs over, the one named last changes fastest.
Arguments:
- latents: bfloat16 [16, 1024, 1024], P('dp', 'mp'), may hold values from -6 to 6
- condition: bfloat16 [16, 1024], P('dp'), may hold values from -6 to 6
- modulation_weight: bfloat16 [1024, 6, 1024], P('dp', None, 'mp'), may hold values from -0.1875 to 0.1875
- modulation_bias: bfloat16 [6, 1024], P(None, ('mp', 'dp')), may hold values from -3 to 3
- query_key_value_weight: bfloat16 [1024, 3, 1024], P('dp', None, 'mp'), may hold values from -0.1875 to 0.1875
- query_value_bias: bfloat16 [2, 1024], P(None, ('mp', 'dp')), may hold values from -3 to 3
- attention_output_weight: bfloat16 [1024, 1024], P('mp', 'dp'), may hold values from -1.5 to 1.5
- up_projection_weight: bfloat16 [1024, 4096], P('dp', 'mp'), may hold values from -0.1875 to 0.1875
- up_projection_bias: bfloat16 [4096], P(('mp', 'dp')), may hold values from -3 to 3
- down_projection_weight: bfloat16 [4096, 1024], P('mp', 'dp'), may hold values from -0.09375 to 0.09375
- projection_row_bias: bfloat16 [2, 1024], P(None, ('mp', 'dp')), may hold values from -3 to 3
- cotangent: bfloat16 [16, 1024, 1024], P('dp', 'mp'), may hold values from -6 to 6
Outputs:
- output: bfloat16 [16, 1024, 1024], P('dp', 'mp')
- latents_grad: bfloat16 [16, 1024, 1024], P('dp', 'mp')
- condition_grad: bfloat16 [16, 1024], P('dp', 'mp')
- mod_weight_grad: float32 [1024, 6, 1024], P('dp', None, 'mp')
- mod_bias_grad: float32 [6, 1024], P(None, ('mp', 'dp'))
- qkv_weight_grad: float32 [1024, 3, 1024], P('dp', None, 'mp')
- qv_bias_grad: float32 [2, 1024], P(None, ('mp', 'dp'))
- out_weight_grad: float32 [1024, 1024], P('mp', 'dp')
- up_weight_grad: float32 [1024, 4096], P('dp', 'mp')
- up_bias_grad: float32 [4096], P(('mp', 'dp'))
- down_weight_grad: float32 [4096, 1024], P('mp', 'dp')
- row_bias_grad: float32 [2, 1024], P(None, ('mp', 'dp'))
All inputs are finite; a program needn't handle non-finite values.
Results may differ from a plain program's by a relative error of at most 0.02.
The roundings to bfloat16 on the way count: a program that leaves them out, or rounds other values in their place, can miss the bound.
Values may be sent and summed in bfloat16 or wider, within the bound.
A program may use at most 192 MiB of HBM per device.

v0:
```python
import jax
import jax.numpy as jnp
from jax import lax
from jax.sharding import PartitionSpec as P

HEAD_DIM = 64


epsilon = 1e-06
precise = lax.Precision.HIGHEST


def layer_norm(values):
    center = values - jnp.mean(values, axis=-1, keepdims=True)
    inverse = lax.rsqrt(jnp.mean(center * center, axis=-1, keepdims=True) + epsilon)
    return (center * inverse, inverse)


def norm_back(grad_normed, normed, inverse):
    first = jnp.mean(grad_normed, axis=-1, keepdims=True)
    second = jnp.mean(grad_normed * normed, axis=-1, keepdims=True)
    return inverse * (grad_normed - first - normed * second)


def gelu_tanh(values):
    return jax.nn.gelu(values, approximate=True)


def local(
    latents,
    condition,
    modulation_weight,
    modulation_bias,
    query_key_value_weight,
    query_value_bias,
    attention_output_weight,
    up_projection_weight,
    up_projection_bias,
    down_projection_weight,
    projection_row_bias,
    cotangent,
):
    mp_count = lax.axis_size("mp")
    model_width = latents.shape[2]
    slice_width = model_width // mp_count
    offset = lax.axis_index("mp") * slice_width
    gathered = (
        lax.all_gather(modulation_weight, "dp", axis=0, tiled=True),
        lax.all_gather(modulation_bias, "dp", axis=1, tiled=True),
        lax.all_gather(query_key_value_weight, "dp", axis=0, tiled=True),
        lax.all_gather(query_value_bias, "dp", axis=1, tiled=True),
        lax.all_gather(attention_output_weight, "dp", axis=1, tiled=True),
        lax.all_gather(up_projection_weight, "dp", axis=0, tiled=True),
        lax.all_gather(up_projection_bias, "dp", axis=0, tiled=True),
        lax.all_gather(down_projection_weight, "dp", axis=1, tiled=True),
        lax.all_gather(projection_row_bias, "dp", axis=1, tiled=True),
    )
    (
        mod_matrix,
        mod_offset,
        qkv_matrix,
        qv_offset,
        out_matrix,
        up_matrix,
        up_offset,
        down_matrix,
        row_offset,
    ) = gathered
    tokens_in = jnp.swapaxes(latents, 0, 1).astype(jnp.float32)
    cond_float = condition.astype(jnp.float32)
    activated = jax.nn.silu(cond_float).astype(jnp.bfloat16)
    mod_part = jnp.einsum(
        "sd,dkf->skf", activated, mod_matrix, preferred_element_type=jnp.float32
    ) + mod_offset.astype(jnp.float32)
    modulation = lax.all_gather(mod_part, "mp", axis=2, tiled=True)
    shift_attn = modulation[:, 0]
    scale_attn = modulation[:, 1]
    gate_attn = modulation[:, 2]
    shift_mlp = modulation[:, 3]
    scale_mlp = modulation[:, 4]
    gate_mlp = modulation[:, 5]
    normed_a, inverse_a = layer_norm(tokens_in)
    input_a = (normed_a * (1.0 + scale_attn) + shift_attn).astype(jnp.bfloat16)
    input_a_full = lax.all_gather(input_a, "mp", axis=0, tiled=True)
    seq_full = input_a_full.shape[0]
    batch_size = input_a_full.shape[1]
    qkv_shift = jnp.stack([qv_offset[0], jnp.zeros_like(qv_offset[0]), qv_offset[1]]).astype(
        jnp.float32
    )
    qkv_all = (
        jnp.einsum("tsd,dkf->tskf", input_a_full, qkv_matrix, preferred_element_type=jnp.float32)
        + qkv_shift
    ).astype(jnp.bfloat16)
    heads_local = slice_width // HEAD_DIM
    shape_heads = (seq_full, batch_size, heads_local, HEAD_DIM)
    queries = qkv_all[:, :, 0].reshape(shape_heads)
    keys_all = qkv_all[:, :, 1].reshape(shape_heads)
    values_all = qkv_all[:, :, 2].reshape(shape_heads)
    temper = HEAD_DIM ** (-0.5)
    block_rows = min(512, seq_full)
    blocks = seq_full // block_rows
    query_blocks = queries.reshape((blocks, block_rows) + shape_heads[1:])

    def attend(query_block):
        scores = (
            jnp.einsum("qshe,kshe->shqk", query_block, keys_all, preferred_element_type=jnp.float32)
            * temper
        )
        maximum = jnp.max(scores, axis=-1, keepdims=True)
        exponent = jnp.exp(scores - maximum)
        denominator = jnp.sum(exponent, axis=-1, keepdims=True)
        attention = (exponent / denominator).astype(jnp.bfloat16)
        layer_output = jnp.einsum(
            "shqk,kshe->qshe", attention, values_all, preferred_element_type=jnp.float32
        )
        return (layer_output.astype(jnp.bfloat16), (maximum + jnp.log(denominator))[..., 0])

    attended_blocks, logsum = lax.map(attend, query_blocks)
    attended = attended_blocks.reshape(seq_full, batch_size, slice_width)
    row_full = lax.dynamic_update_slice(
        jnp.zeros((2, model_width), jnp.float32),
        row_offset.astype(jnp.float32),
        (jnp.zeros((), jnp.int32), offset),
    )
    row_block = attended
    branch_attn = lax.psum_scatter(
        (
            jnp.einsum("tsf,fd->tsd", row_block, out_matrix, preferred_element_type=jnp.float32)
            + row_full[0]
        ).astype(jnp.bfloat16),
        "mp",
        scatter_dimension=0,
        tiled=True,
    ).astype(jnp.float32)
    middle = tokens_in + gate_attn * branch_attn
    normed_m, inverse_m = layer_norm(middle)
    input_m = (normed_m * (1.0 + scale_mlp) + shift_mlp).astype(jnp.bfloat16)
    input_m_full = lax.all_gather(input_m, "mp", axis=0, tiled=True)
    pre_up = jnp.einsum(
        "tsd,df->tsf", input_m_full, up_matrix, preferred_element_type=jnp.float32
    ) + up_offset.astype(jnp.float32)
    hidden = gelu_tanh(pre_up).astype(jnp.bfloat16)
    row_block = hidden
    branch_mlp = lax.psum_scatter(
        (
            jnp.einsum("tsf,fd->tsd", row_block, down_matrix, preferred_element_type=jnp.float32)
            + row_full[1]
        ).astype(jnp.bfloat16),
        "mp",
        scatter_dimension=0,
        tiled=True,
    ).astype(jnp.float32)
    result_out = middle + gate_mlp * branch_mlp
    regathered = (
        lax.all_gather(modulation_weight, "dp", axis=0, tiled=True),
        lax.all_gather(modulation_bias, "dp", axis=1, tiled=True),
        lax.all_gather(query_key_value_weight, "dp", axis=0, tiled=True),
        lax.all_gather(query_value_bias, "dp", axis=1, tiled=True),
        lax.all_gather(attention_output_weight, "dp", axis=1, tiled=True),
        lax.all_gather(up_projection_weight, "dp", axis=0, tiled=True),
        lax.all_gather(up_projection_bias, "dp", axis=0, tiled=True),
        lax.all_gather(down_projection_weight, "dp", axis=1, tiled=True),
        lax.all_gather(projection_row_bias, "dp", axis=1, tiled=True),
    )
    mod_matrix = regathered[0]
    qkv_matrix = regathered[2]
    out_matrix = regathered[4]
    up_matrix = regathered[5]
    down_matrix = regathered[7]
    grad_out = jnp.swapaxes(cotangent, 0, 1).astype(jnp.float32)
    grad_gate_mlp = jnp.sum(grad_out * branch_mlp, axis=0)
    grad_branch_mlp = (gate_mlp * grad_out).astype(jnp.bfloat16)
    grad_mlp_full = lax.all_gather(grad_branch_mlp, "mp", axis=0, tiled=True)
    down_grad = jnp.einsum("tsf,tsd->fd", hidden, grad_mlp_full, preferred_element_type=jnp.float32)
    column_mlp = lax.dynamic_slice_in_dim(
        jnp.sum(grad_mlp_full, axis=(0, 1), dtype=jnp.float32), offset, slice_width
    )
    grad_hidden = jnp.einsum(
        "tsd,fd->tsf", grad_mlp_full, down_matrix, preferred_element_type=jnp.float32
    )
    unused_gelu, gelu_back = jax.vjp(gelu_tanh, pre_up)
    grad_pre_up = gelu_back(grad_hidden)[0].astype(jnp.bfloat16)
    up_grad = jnp.einsum(
        "tsd,tsf->df", input_m_full, grad_pre_up, preferred_element_type=jnp.float32
    )
    up_bias_part = jnp.sum(grad_pre_up, axis=(0, 1), dtype=jnp.float32)
    row_block = grad_pre_up
    grad_input_m = lax.psum_scatter(
        jnp.einsum("tsf,df->tsd", row_block, up_matrix, preferred_element_type=jnp.float32).astype(
            jnp.bfloat16
        ),
        "mp",
        scatter_dimension=0,
        tiled=True,
    ).astype(jnp.float32)
    grad_shift_mlp = jnp.sum(grad_input_m, axis=0)
    grad_scale_mlp = jnp.sum(grad_input_m * normed_m, axis=0)
    grad_middle = grad_out + norm_back(grad_input_m * (1.0 + scale_mlp), normed_m, inverse_m)
    grad_gate_attn = jnp.sum(grad_middle * branch_attn, axis=0)
    grad_branch_attn = (gate_attn * grad_middle).astype(jnp.bfloat16)
    grad_attn_full = lax.all_gather(grad_branch_attn, "mp", axis=0, tiled=True)
    out_grad = jnp.einsum(
        "tsf,tsd->fd", attended, grad_attn_full, preferred_element_type=jnp.float32
    )
    column_attn = lax.dynamic_slice_in_dim(
        jnp.sum(grad_attn_full, axis=(0, 1), dtype=jnp.float32), offset, slice_width
    )
    grad_attended = jnp.einsum(
        "tsd,fd->tsf", grad_attn_full, out_matrix, preferred_element_type=jnp.float32
    ).astype(jnp.bfloat16)
    grad_blocks = grad_attended.reshape((blocks, block_rows) + shape_heads[1:])

    def attend_back(running, inputs):
        query_block, grad_block, logsum_block = inputs
        scores = (
            jnp.einsum("qshe,kshe->shqk", query_block, keys_all, preferred_element_type=jnp.float32)
            * temper
        )
        attention = jnp.exp(scores - logsum_block[..., None])
        grad_attention = jnp.einsum(
            "qshe,kshe->shqk", grad_block, values_all, preferred_element_type=jnp.float32
        )
        inner_sum = jnp.sum(attention * grad_attention, axis=-1, keepdims=True)
        grad_scores = (attention * (grad_attention - inner_sum)).astype(jnp.bfloat16)
        grad_query = (
            jnp.einsum("shqk,kshe->qshe", grad_scores, keys_all, preferred_element_type=jnp.float32)
            * temper
        )
        grad_key = (
            jnp.einsum(
                "shqk,qshe->kshe", grad_scores, query_block, preferred_element_type=jnp.float32
            )
            * temper
        )
        grad_value = jnp.einsum(
            "shqk,qshe->kshe",
            attention.astype(jnp.bfloat16),
            grad_block,
            preferred_element_type=jnp.float32,
        )
        return ((running[0] + grad_key, running[1] + grad_value), grad_query)

    initial = (jnp.zeros(shape_heads, jnp.float32), jnp.zeros(shape_heads, jnp.float32))
    (grad_keys, grad_values), grad_queries = lax.scan(
        attend_back, initial, (query_blocks, grad_blocks, logsum)
    )
    flat_shape = (seq_full, batch_size, slice_width)
    grad_qkv = jnp.stack(
        [
            grad_queries.reshape(flat_shape),
            grad_keys.reshape(flat_shape),
            grad_values.reshape(flat_shape),
        ],
        axis=2,
    ).astype(jnp.bfloat16)
    qkv_grad = jnp.einsum(
        "tsd,tskf->dkf", input_a_full, grad_qkv, preferred_element_type=jnp.float32
    )
    qv_bias_part = jnp.stack(
        [
            jnp.sum(grad_qkv[:, :, 0], axis=(0, 1), dtype=jnp.float32),
            jnp.sum(grad_qkv[:, :, 2], axis=(0, 1), dtype=jnp.float32),
        ]
    )
    row_block = grad_qkv
    grad_input_a = lax.psum_scatter(
        jnp.einsum(
            "tskf,dkf->tsd", row_block, qkv_matrix, preferred_element_type=jnp.float32
        ).astype(jnp.bfloat16),
        "mp",
        scatter_dimension=0,
        tiled=True,
    ).astype(jnp.float32)
    grad_shift_attn = jnp.sum(grad_input_a, axis=0)
    grad_scale_attn = jnp.sum(grad_input_a * normed_a, axis=0)
    grad_tokens = grad_middle + norm_back(grad_input_a * (1.0 + scale_attn), normed_a, inverse_a)
    grad_mod_full = jnp.stack(
        [
            grad_shift_attn,
            grad_scale_attn,
            grad_gate_attn,
            grad_shift_mlp,
            grad_scale_mlp,
            grad_gate_mlp,
        ],
        axis=1,
    )
    grad_mod = lax.psum_scatter(grad_mod_full, "mp", scatter_dimension=2, tiled=True)
    mod_bias_part = jnp.sum(grad_mod, axis=0)
    mod_grad = jnp.einsum("sd,skf->dkf", activated.astype(jnp.float32), grad_mod, precision=precise)
    grad_activated = jnp.einsum(
        "skf,dkf->sd", grad_mod, mod_matrix.astype(jnp.float32), precision=precise
    )
    unused_silu, silu_back = jax.vjp(jax.nn.silu, cond_float)
    cond_part = silu_back(grad_activated)[0]
    cond_grad = lax.psum_scatter(cond_part, "mp", scatter_dimension=1, tiled=True)
    row_bias_part = jnp.stack([column_attn, column_mlp])
    reduced = (
        lax.psum_scatter(
            mod_grad.astype(jnp.bfloat16), "dp", scatter_dimension=0, tiled=True
        ).astype(jnp.float32),
        lax.psum_scatter(
            mod_bias_part.astype(jnp.bfloat16), "dp", scatter_dimension=1, tiled=True
        ).astype(jnp.float32),
        lax.psum_scatter(
            qkv_grad.astype(jnp.bfloat16), "dp", scatter_dimension=0, tiled=True
        ).astype(jnp.float32),
        lax.psum_scatter(
            qv_bias_part.astype(jnp.bfloat16), "dp", scatter_dimension=1, tiled=True
        ).astype(jnp.float32),
        lax.psum_scatter(
            out_grad.astype(jnp.bfloat16), "dp", scatter_dimension=1, tiled=True
        ).astype(jnp.float32),
        lax.psum_scatter(
            up_grad.astype(jnp.bfloat16), "dp", scatter_dimension=0, tiled=True
        ).astype(jnp.float32),
        lax.psum_scatter(
            up_bias_part.astype(jnp.bfloat16), "dp", scatter_dimension=0, tiled=True
        ).astype(jnp.float32),
        lax.psum_scatter(
            down_grad.astype(jnp.bfloat16), "dp", scatter_dimension=1, tiled=True
        ).astype(jnp.float32),
        lax.psum_scatter(
            row_bias_part.astype(jnp.bfloat16), "dp", scatter_dimension=1, tiled=True
        ).astype(jnp.float32),
    )
    leading = (
        jnp.swapaxes(result_out, 0, 1).astype(jnp.bfloat16),
        jnp.swapaxes(grad_tokens, 0, 1).astype(jnp.bfloat16),
        cond_grad.astype(jnp.bfloat16),
    )
    return leading + tuple(reduced)


def solution(mesh):
    placed = (
        P("dp", "mp", None),
        P("dp", None),
        P("dp", None, "mp"),
        P(None, ("mp", "dp")),
        P("dp", None, "mp"),
        P(None, ("mp", "dp")),
        P("mp", "dp"),
        P("dp", "mp"),
        P(("mp", "dp")),
        P("mp", "dp"),
        P(None, ("mp", "dp")),
        P("dp", "mp", None),
    )
    return jax.shard_map(
        local,
        mesh=mesh,
        in_specs=placed,
        out_specs=(
            P("dp", "mp", None),
            P("dp", "mp", None),
            P("dp", "mp"),
            P("dp", None, "mp"),
            P(None, ("mp", "dp")),
            P("dp", None, "mp"),
            P(None, ("mp", "dp")),
            P("mp", "dp"),
            P("dp", "mp"),
            P(("mp", "dp")),
            P("mp", "dp"),
            P(None, ("mp", "dp")),
        ),
        check_vma=False,
    )
```

profile of v0, /device:TPU:0, one launch (start us, length us, event | category | flops | bytes accessed | tf_op | source)
XLA Modules:
  0.0 1247.7 jit_solution(8100953531234236413)
XLA Ops:
  8.7 23.6 %all-gather.1 = bf16[16,32,6]{1,2,0:T(8,128)(2,1)S(1)} all-gather(bf16[1,32,6]{1,2,0:T(8,128)(2,1)} %bitcast.351), channel_id=1, replica_groups=mesh['dp'=16,'mp'=2] {'dp'}, dimensions={0}, use_global_device_ids=true | all-gather | bytes 6528 | tf_op jit(solution)/shard_map/all_gather | solution.py:49
  35.5 39.4 %all-gather.15.cloned.1.call-done = bf16[1024,6,512]{2,0,1:T(8,128)(2,1)} async-done(((bf16[64,6,512]{2,0,1:T(8,128)(2,1)}), bf16[1024,6,512]{2,0,1:T(8,128)(2,1)}) %all-gather.15.cloned.1.call-update) | async-done | bytes 6291472 | tf_op jit(solution)/shard_map/all_gather | solution.py:48
  74.9 3.7 fusion.106
  78.7 4.5 all-gather
  85.9 19.0 %all-gather.2 = bf16[16,32,2]{1,2,0:T(2,128)(2,1)S(1)} all-gather(bf16[1,32,2]{1,2,0:T(2,128)(2,1)S(1)} %bitcast.352), channel_id=1, replica_groups=mesh['dp'=16,'mp'=2] {'dp'}, dimensions={0}, use_global_device_ids=true | all-gather | bytes 2176 | tf_op jit(solution)/shard_map/all_gather | solution.py:51
  105.1 17.8 %all-gather.3 = bf16[16,32,2]{1,2,0:T(2,128)(2,1)S(1)} all-gather(bf16[1,32,2]{1,2,0:T(2,128)(2,1)S(1)} %bitcast.353), channel_id=1, replica_groups=mesh['dp'=16,'mp'=2] {'dp'}, dimensions={0}, use_global_device_ids=true | all-gather | bytes 2176 | tf_op jit(solution)/shard_map/all_gather | solution.py:56
  123.8 31.6 %all-gather.17.cloned.1.call-done = bf16[1024,1,1024]{2,0,1:T(8,128)(2,1)} async-done(((bf16[512,1,1024]{2,0,1:T(8,128)(2,1)}), bf16[1024,1,1024]{2,0,1:T(8,128)(2,1)}) %all-gather.17.cloned.1.call-update) | async-done | bytes 2097168 | tf_op jit(solution)/shard_map/all_gather | solution.py:84
  155.3 6.0 fusion.46
  164.7 22.5 %while.27 = (s32[]{:T(128)}, bf16[2,512,1,8,64]{1,4,3,2,0:T(8,128)(2,1)}, f32[2,1,8,512]{3,2,1,0:T(8,128)S(1)}, bf16[2,512,1,8,64]{1,4,3,2,0:T(8,128)(2,1)S(1)},...) while((s32[]{:T(128)}, bf16[2,512,1,8,64]{1,4,3,2,0:T(8,128)(2,1)}, ...), condition=%wide.region_5.6_spmd, body=%wide.region_2.5_spmd.sunk | while | flops 1111748608 | bytes 61997208 | solution.py:118
  164.7 2.5 multiply_reduce_fusion.5
  167.1 3.4 fusion.149
  170.6 4.3 fusion.150
  175.9 2.5 multiply_reduce_fusion.5
  178.4 3.4 fusion.149
  181.9 4.3 fusion.150
  187.2 2.7 copy.60
  191.1 4.2 all-gather.21.cloned.1.call-done
  195.3 4.3 fusion.92
  200.4 30.1 %reduce-scatter.23.cloned.1.call-done = bf16[512,1,1024]{2,0,1:T(8,128)(2,1)} async-done(((bf16[1024,1,1024]{2,0,1:T(8,128)(2,1)}), bf16[512,1,1024]{2,0,1:T(8,128)(2,1)}) %reduce-scatter.23.cloned.1.call-update) | async-done | bytes 1048592 | tf_op jit(solution)/shard_map/reduce_scatter | solution.py:126
  236.6 2.5 fusion.75
  239.1 21.2 %all-gather.4 = bf16[16,1,128]{2,1,0:T(2,128)(2,1)S(1)} all-gather(bf16[1,1,128]{2,1,0:T(2,128)(2,1)S(1)} %bitcast.354), channel_id=1, replica_groups=mesh['dp'=16,'mp'=2] {'dp'}, dimensions={0}, use_global_device_ids=true | all-gather | bytes 4352 | tf_op jit(solution)/shard_map/all_gather | solution.py:54
  260.4 23.0 %all-gather.25.cloned.1.call-done = bf16[1024,2048]{1,0:T(8,128)(2,1)} async-done(((bf16[64,2048]{1,0:T(8,128)(2,1)}), bf16[1024,2048]{1,0:T(8,128)(2,1)}) %all-gather.25.cloned.1.call-update) | async-done | bytes 4194320 | tf_op jit(solution)/shard_map/all_gather | solution.py:53
  283.4 33.8 %all-gather.23.cloned.1.call-done = bf16[1024,1,1024]{2,0,1:T(8,128)(2,1)} async-done(((bf16[512,1,1024]{2,0,1:T(8,128)(2,1)}), bf16[1024,1,1024]{2,0,1:T(8,128)(2,1)}) %all-gather.23.cloned.1.call-update) | async-done | bytes 2097168 | tf_op jit(solution)/shard_map/all_gather | solution.py:138
  317.2 10.5 fusion.88
  327.8 42.5 %all-gather.27.cloned.1.call-done = bf16[2048,1024]{0,1:T(8,128)(2,1)} async-done(((bf16[2048,64]{0,1:T(8,128)(2,1)}), bf16[2048,1024]{0,1:T(8,128)(2,1)}) %all-gather.27.cloned.1.call-update) | async-done | bytes 4194320 | tf_op jit(solution)/shard_map/all_gather | solution.py:55
  370.2 33.3 %all-gather.29.cloned.1.call-done = bf16[1024,1,1024]{2,0,1:T(8,128)(2,1)} async-done(((bf16[512,1,1024]{2,0,1:T(8,128)(2,1)}), bf16[1024,1,1024]{2,0,1:T(8,128)(2,1)}) %all-gather.29.cloned.1.call-update) | async-done | bytes 2097168 | tf_op jit(solution)/shard_map/all_gather | solution.py:173
  403.5 13.7 %fusion.118 = (bf16[2048]{0:T(1024)(128)(2,1)}, bf16[1024,2048]{1,0:T(8,128)(2,1)S(1)}) fusion(f32[1024,2048]{1,0:T(8,128)} %fusion.88, f32[2048]{0:T(1024)S(1)} %bitcast.344, bf16[2048,1024]{0,1:T(8,128)(2,1)} %all-gather.27.cloned.1.call-done, bf16[1024,1,1024]{2,0,1:T(8,128)(2,1)} %all-gather.29.cloned.1.call-done), kind=kOutput, calls=%fused_computation.177 | convolution fusion | flops 4341102592 | bytes 18886656 | tf_op jit(solution)/shard_map/tsd,fd->tsf/dot_general | solution.py:178
  419.2 5.7 convert_bitcast_fusion.1
  425.3 11.4 fusion.77
  436.7 20.3 %reduce-scatter.27.cloned.1.call-done = bf16[512,1,1024]{2,0,1:T(8,128)(2,1)} async-done(((bf16[1024,1,1024]{2,0,1:T(8,128)(2,1)}), bf16[512,1,1024]{2,0,1:T(8,128)(2,1)}) %reduce-scatter.27.cloned.1.call-update) | async-done | bytes 1048592 | tf_op jit(solution)/shard_map/reduce_scatter | solution.py:188
  457.0 3.3 fusion.73
  460.3 30.8 %reduce-scatter.25.cloned.1.call-done = bf16[512,1,1024]{2,0,1:T(8,128)(2,1)} async-done(((bf16[1024,1,1024]{2,0,1:T(8,128)(2,1)}), bf16[512,1,1024]{2,0,1:T(8,128)(2,1)}) %reduce-scatter.25.cloned.1.call-update) | async-done | bytes 1048592 | tf_op jit(solution)/shard_map/reduce_scatter | solution.py:144
  491.1 4.8 fusion.66
  498.6 33.2 %all-gather.31.cloned.1.call-done = bf16[1024,1,1024]{2,0,1:T(8,128)(2,1)} async-done(((bf16[512,1,1024]{2,0,1:T(8,128)(2,1)}), bf16[1024,1,1024]{2,0,1:T(8,128)(2,1)}) %all-gather.31.cloned.1.call-update) | async-done | bytes 2097168 | tf_op jit(solution)/shard_map/all_gather | solution.py:201
  531.8 3.1 fusion.94
  534.9 2.5 reshape.840
  537.4 3.3 copy.64
  540.7 75.1 %while.28 = (s32[]{:T(128)}, f32[1024,1,8,64]{0,3,2,1:T(8,128)}, f32[1024,1,8,64]{0,3,2,1:T(8,128)}, bf16[2,512,1,8,64]{1,4,3,2,0:T(8,128)(2,1)}, bf16[2,512,1,8...) while((s32[]{:T(128)}, f32[1024,1,8,64]{0,3,2,1:T(8,128)}, ...), condition=%wide.region_15.16_spmd.clone, body=%wide.region_13.15_spmd.clone.sunk | while | flops 2737565696 | bytes 195150096 | solution.py:244
  543.1 4.4 bitcast_add_fusion.6
  547.5 9.6 multiply_reduce_fusion.6
  557.1 10.4 multiply_convert_fusion.7
  567.5 7.0 fusion.160
  580.0 5.6 bitcast_add_fusion.6
  585.7 9.6 multiply_reduce_fusion.6
  595.2 10.4 multiply_convert_fusion.7
  605.7 7.0 fusion.160
  626.1 7.4 fusion.93
  633.7 31.9 %reduce-scatter.29.cloned.1.call-done = bf16[512,1,1024]{2,0,1:T(8,128)(2,1)} async-done(((bf16[1024,1,1024]{2,0,1:T(8,128)(2,1)}), bf16[512,1,1024]{2,0,1:T(8,128)(2,1)}) %reduce-scatter.29.cloned.1.call-update) | async-done | bytes 1048592 | tf_op jit(solution)/shard_map/reduce_scatter | solution.py:266
  668.6 10.8 convolution_convert_fusion
  679.7 9.3 convolution_convert_fusion.1
  695.7 4.3 fusion.97
  700.2 8.1 fusion.105
  710.5 7.6 convolution_convert_fusion.2
  718.2 4.6 multiply_convert_fusion.1
  724.8 33.4 %all-reduce = bf16[2048]{0:T(1024)(128)(2,1)S(1)} all-reduce(bf16[2048]{0:T(1024)(128)(2,1)S(1)} %copy-done.34), channel_id=15, replica_groups=mesh['dp'=16,'mp'=2] {'dp'}, use_global_device_ids=true, to_apply=%region_36.37.clone | all-reduce | flops 2048 | bytes 8192
  760.5 70.3 %reduce-scatter.39.cloned.1.call-done = bf16[64,2048]{1,0:T(8,128)(2,1)} async-done(((bf16[1024,2048]{1,0:T(8,128)(2,1)}), bf16[64,2048]{1,0:T(8,128)(2,1)}) %reduce-scatter.39.cloned.1.call-update) | async-done | bytes 262160 | tf_op jit(solution)/shard_map/reduce_scatter | solution.py:314
  832.6 55.6 %reduce-scatter.49.cloned.1.call-done = bf16[32,2]{1,0:T(8,128)(2,1)} async-done(((bf16[512,2]{1,0:T(8,128)(2,1)}), bf16[32,2]{1,0:T(8,128)(2,1)}) %reduce-scatter.49.cloned.1.call-update) | async-done | bytes 144
  889.6 56.7 %reduce-scatter.47.cloned.1.call-done = bf16[32,2]{1,0:T(8,128)(2,1)} async-done(((bf16[512,2]{1,0:T(8,128)(2,1)}), bf16[32,2]{1,0:T(8,128)(2,1)}) %reduce-scatter.47.cloned.1.call-update) | async-done | bytes 144
  947.6 58.7 %reduce-scatter.37.cloned.1.call-done = bf16[512,64]{0,1:T(8,128)(2,1)} async-done(((bf16[512,1024]{0,1:T(8,128)(2,1)}), bf16[512,64]{0,1:T(8,128)(2,1)}) %reduce-scatter.37.cloned.1.call-update) | async-done | bytes 65552 | tf_op jit(solution)/shard_map/reduce_scatter | solution.py:311
  1007.8 3.3 fusion.101
  1011.1 11.6 reduce-scatter.43.cloned.1.call-done
  1024.3 57.5 %reduce-scatter.45.cloned.1.call-done = bf16[32,6]{1,0:T(8,128)(2,1)} async-done(((bf16[512,6]{1,0:T(8,128)(2,1)}), bf16[32,6]{1,0:T(8,128)(2,1)}) %reduce-scatter.45.cloned.1.call-update) | async-done | bytes 400
  1083.2 67.6 %reduce-scatter.35.cloned.1.call-done = bf16[64,3,512]{2,0,1:T(8,128)(2,1)} async-done(((bf16[1024,3,512]{2,0,1:T(8,128)(2,1)}), bf16[64,3,512]{2,0,1:T(8,128)(2,1)}) %reduce-scatter.35.cloned.1.call-update) | async-done | bytes 196624 | tf_op jit(solution)/shard_map/reduce_scatter | solution.py:305
  1152.5 86.4 %reduce-scatter.33.cloned.1.call-done = bf16[64,6,512]{2,0,1:T(8,128)(2,1)} async-done(((bf16[1024,6,512]{2,0,1:T(8,128)(2,1)}), bf16[64,6,512]{2,0,1:T(8,128)(2,1)}) %reduce-scatter.33.cloned.1.call-update) | async-done | bytes 393232 | tf_op jit(solution)/shard_map/reduce_scatter | solution.py:299
  (233 shorter events, 76.5 us)
Async XLA Ops:
  7.2 67.7 %all-gather.15.cloned.1.call-start = ((), (), s32[]{:S(2)}) async-start(), calls=%async_computation.14 | async-start | bytes 6684672 | tf_op jit(solution)/shard_map/all_gather | solution.py:48
  7.9 115.9 %all-gather.19.cloned.1.call-start = ((), (), s32[]{:S(2)}) async-start(), calls=%async_computation.16 | async-start | bytes 3342336 | tf_op jit(solution)/shard_map/all_gather | solution.py:50
  8.7 146.7 %all-gather.17.cloned.1.call-start = ((), (), s32[]{:S(2)}) async-start(), calls=%async_computation.15 | async-start | bytes 3145728 | tf_op jit(solution)/shard_map/all_gather | solution.py:84
  33.8 50.0 %copy-start.21 = (f32[512]{0:T(512)}, f32[512]{0:T(512)S(1)}, u32[]{:S(2)}) copy-start(f32[512]{0:T(512)S(1)} %broadcast_multiply_fusion.5) | copy-start | bytes 6148
  35.5 48.4 %copy-start.25 = (f32[512]{0:T(512)}, f32[512]{0:T(512)S(1)}, u32[]{:S(2)}) copy-start(f32[512]{0:T(512)S(1)} %add_rsqrt_fusion.1) | copy-start | bytes 6148
  35.5 48.4 %copy-start.3 = (bf16[1,512,1024]{2,1,0:T(8,128)(2,1)S(1)}, bf16[1,512,1024]{2,1,0:T(8,128)(2,1)}, u32[]{:S(2)}) copy-start(bf16[1,512,1024]{2,1,0:T(8,128)(2,1)} %param.16) | copy-start | bytes 3145732
  78.6 7.3 copy-start.37
  78.6 26.4 %copy-start.38 = (bf16[2,32]{1,0:T(2,128)(2,1)S(1)}, bf16[2,32]{1,0:T(2,128)(2,1)}, u32[]{:S(2)}) copy-start(bf16[2,32]{1,0:T(2,128)(2,1)} %param.26) | copy-start | bytes 388
  83.8 71.5 %copy-start.19 = (f32[1,1,1024]{2,1,0:T(1,128)}, f32[1,1,1024]{2,1,0:T(1,128)S(1)}, u32[]{:S(2)}) copy-start(f32[1,1,1024]{2,1,0:T(1,128)S(1)} %get-tuple-element.244) | copy-start | bytes 12292
  85.3 110.0 %all-gather.21.cloned.1.call-start = ((), (), s32[]{:S(2)}) async-start(), calls=%async_computation.17 | async-start | bytes 1114112 | tf_op jit(solution)/shard_map/all_gather | solution.py:52
  85.9 144.7 %reduce-scatter.23.cloned.1.call-start = ((), (), s32[]{:S(2)}) async-start(), calls=%async_computation.18 | async-start | bytes 3145728 | tf_op jit(solution)/shard_map/reduce_scatter | solution.py:126
  167.1 3.5 copy-start.14
  178.4 3.5 copy-start.14
  187.2 8.1 copy-start.7
  187.2 8.1 copy-start.36
  195.3 35.2 %copy-start.4 = (bf16[1,512,1024]{2,1,0:T(8,128)(2,1)S(1)}, bf16[1,512,1024]{2,1,0:T(8,128)(2,1)}, u32[]{:S(2)}) copy-start(bf16[1,512,1024]{2,1,0:T(8,128)(2,1)} %param.16) | copy-start | bytes 3145732
  195.3 35.2 %copy-start.16 = (f32[1,1,1024]{2,1,0:T(1,128)S(1)}, f32[1,1,1024]{2,1,0:T(1,128)}, u32[]{:S(2)}) copy-start(f32[1,1,1024]{2,1,0:T(1,128)} %get-tuple-element.245) | copy-start | bytes 12292
  199.6 34.5 %copy-start.18 = (f32[1,1,1024]{2,1,0:T(1,128)S(1)}, f32[1,1,1024]{2,1,0:T(1,128)}, u32[]{:S(2)}) copy-start(f32[1,1,1024]{2,1,0:T(1,128)} %get-tuple-element.242) | copy-start | bytes 12292
  199.6 34.5 %copy-start.31 = (f32[1,1,1024]{2,1,0:T(1,128)S(1)}, f32[1,1,1024]{2,1,0:T(1,128)}, u32[]{:S(2)}) copy-start(f32[1,1,1024]{2,1,0:T(1,128)} %get-tuple-element.241) | copy-start | bytes 12292
  199.6 83.8 %all-gather.25.cloned.1.call-start = ((), (), s32[]{:S(2)}) async-start(), calls=%async_computation.20 | async-start | bytes 4456448 | tf_op jit(solution)/shard_map/all_gather | solution.py:53
  200.2 117.0 %all-gather.23.cloned.1.call-start = ((), (), s32[]{:S(2)}) async-start(), calls=%async_computation.19 | async-start | bytes 3145728 | tf_op jit(solution)/shard_map/all_gather | solution.py:138
  230.6 3.6 copy-start.8
  232.3 4.3 copy-start.23
  234.1 5.0 copy-start.39
  235.8 134.5 %all-gather.27.cloned.1.call-start = ((), (), s32[]{:S(2)}) async-start(), calls=%async_computation.21 | async-start | bytes 4456448 | tf_op jit(solution)/shard_map/all_gather | solution.py:55
  236.5 167.0 %all-gather.29.cloned.1.call-start = ((), (), s32[]{:S(2)}) async-start(), calls=%async_computation.23 | async-start | bytes 3145728 | tf_op jit(solution)/shard_map/all_gather | solution.py:173
  239.0 217.9 %reduce-scatter.27.cloned.1.call-start = ((), (), s32[]{:S(2)}) async-start(), calls=%async_computation.24 | async-start | bytes 3145728 | tf_op jit(solution)/shard_map/reduce_scatter | solution.py:188
  260.4 164.9 %copy-start.32 = (f32[16,1,128]{2,1,0:T(1,128)}, f32[16,1,128]{2,1,0:T(1,128)S(1)}, u32[]{:S(2)}) copy-start(f32[16,1,128]{2,1,0:T(1,128)S(1)} %convert_element_type.357) | copy-start | bytes 24580
  403.5 15.7 %copy-start.40 = (bf16[1024,2048]{1,0:T(8,128)(2,1)S(1)}, bf16[1024,2048]{1,0:T(8,128)(2,1)}, u32[]{:S(2)}) copy-start(bf16[1024,2048]{1,0:T(8,128)(2,1)} %all-gather.25.cloned.1.call-done) | copy-start | bytes 12582916
  419.2 6.0 copy-start.35
  425.0 66.1 %reduce-scatter.25.cloned.1.call-start = ((), (), s32[]{:S(2)}) async-start(), calls=%async_computation.22 | async-start | bytes 3145728 | tf_op jit(solution)/shard_map/reduce_scatter | solution.py:144
  436.6 95.1 %all-gather.31.cloned.1.call-start = ((), (), s32[]{:S(2)}) async-start(), calls=%async_computation.25 | async-start | bytes 3145728 | tf_op jit(solution)/shard_map/all_gather | solution.py:201
  498.5 167.1 %reduce-scatter.29.cloned.1.call-start = ((), (), s32[]{:S(2)}) async-start(), calls=%async_computation.26 | async-start | bytes 3145728 | tf_op jit(solution)/shard_map/reduce_scatter | solution.py:266
  540.7 2.4 copy-start.6
  567.5 7.0 copy-start
  567.5 7.0 copy-start.1
  577.7 2.4 copy-start.6
  605.7 7.0 copy-start
  605.7 7.0 copy-start.1
  615.8 3.2 copy-start.10
  622.9 3.2 copy-start.12
  626.1 39.5 %copy-start.5 = (bf16[1,512,1024]{2,1,0:T(8,128)(2,1)S(1)}, bf16[1,512,1024]{2,1,0:T(8,128)(2,1)}, u32[]{:S(2)}) copy-start(bf16[1,512,1024]{2,1,0:T(8,128)(2,1)} %param.16) | copy-start | bytes 3145732
  626.1 39.5 %copy-start.20 = (f32[1,1,1024]{2,1,0:T(1,128)S(1)}, f32[1,1,1024]{2,1,0:T(1,128)}, u32[]{:S(2)}) copy-start(f32[1,1,1024]{2,1,0:T(1,128)} %copy-done.19) | copy-start | bytes 12292
  626.1 39.5 %copy-start.22 = (f32[512]{0:T(512)S(1)}, f32[512]{0:T(512)}, u32[]{:S(2)}) copy-start(f32[512]{0:T(512)} %copy-done.21) | copy-start | bytes 6148
  626.1 39.5 %copy-start.26 = (f32[512]{0:T(512)S(1)}, f32[512]{0:T(512)}, u32[]{:S(2)}) copy-start(f32[512]{0:T(512)} %copy-done.25) | copy-start | bytes 6148
  633.6 34.3 %copy-start.27 = (f32[1024]{0:T(1024)S(1)}, f32[1024]{0:T(1024)}, u32[]{:S(2)}) copy-start(f32[1024]{0:T(1024)} %get-tuple-element.189) | copy-start | bytes 12292
  633.6 34.3 %copy-start.28 = (f32[1024]{0:T(1024)S(1)}, f32[1024]{0:T(1024)}, u32[]{:S(2)}) copy-start(f32[1024]{0:T(1024)} %get-tuple-element.195) | copy-start | bytes 12292
  633.6 34.3 %copy-start.29 = (f32[1024]{0:T(1024)S(1)}, f32[1024]{0:T(1024)}, u32[]{:S(2)}) copy-start(f32[1024]{0:T(1024)} %get-tuple-element.229) | copy-start | bytes 12292
  633.6 34.3 %copy-start.30 = (f32[1024]{0:T(1024)S(1)}, f32[1024]{0:T(1024)}, u32[]{:S(2)}) copy-start(f32[1024]{0:T(1024)} %get-tuple-element.239) | copy-start | bytes 12292
  633.6 35.1 %copy-start.33 = (f32[16,1,128]{2,1,0:T(1,128)S(1)}, f32[16,1,128]{2,1,0:T(1,128)}, u32[]{:S(2)}) copy-start(f32[16,1,128]{2,1,0:T(1,128)} %copy-done.32) | copy-start | bytes 24580
  633.6 66.5 %reduce-scatter.31.cloned.1.call-start = ((), (), s32[]{:S(2)}) async-start(), calls=%async_computation.27 | async-start | bytes 49152 | tf_op jit(solution)/shard_map/reduce_scatter | solution.py:288
  668.6 90.2 %reduce-scatter.41.cloned.1.call-start = ((), (), s32[]{:S(2)}) async-start(), calls=%async_computation.32 | async-start | bytes 4456448 | tf_op jit(solution)/shard_map/reduce_scatter | solution.py:320
  679.5 151.3 %reduce-scatter.39.cloned.1.call-start = ((), (), s32[]{:S(2)}) async-start(), calls=%async_computation.31 | async-start | bytes 4456448 | tf_op jit(solution)/shard_map/reduce_scatter | solution.py:314
  689.1 199.1 %reduce-scatter.49.cloned.1.call-start = ((), (), s32[]{:S(2)}) async-start(), calls=%async_computation.36 | async-start | bytes 139264
  694.7 251.5 %reduce-scatter.47.cloned.1.call-start = ((), (), s32[]{:S(2)}) async-start(), calls=%async_computation.35 | async-start | bytes 139264
  695.6 4.5 copy-start.24
  695.6 310.6 %reduce-scatter.37.cloned.1.call-start = ((), (), s32[]{:S(2)}) async-start(), calls=%async_computation.30 | async-start | bytes 1114112 | tf_op jit(solution)/shard_map/reduce_scatter | solution.py:311
  700.0 322.6 %reduce-scatter.43.cloned.1.call-start = ((), (), s32[]{:S(2)}) async-start(), calls=%async_computation.33 | async-start | bytes 786432
  700.1 9.2 copy-start.17
  700.1 10.4 copy-start.13
  709.3 372.5 %reduce-scatter.45.cloned.1.call-start = ((), (), s32[]{:S(2)}) async-start(), calls=%async_computation.34 | async-start | bytes 139264
  710.2 440.6 %reduce-scatter.35.cloned.1.call-start = ((), (), s32[]{:S(2)}) async-start(), calls=%async_computation.29 | async-start | bytes 3342336 | tf_op jit(solution)/shard_map/reduce_scatter | solution.py:305
  718.1 520.8 %reduce-scatter.33.cloned.1.call-start = ((), (), s32[]{:S(2)}) async-start(), calls=%async_computation.28 | async-start | bytes 6684672 | tf_op jit(solution)/shard_map/reduce_scatter | solution.py:299
  722.9 284.9 %copy-start.11 = (bf16[512,1,1024]{2,0,1:T(8,128)(2,1)S(1)}, bf16[512,1,1024]{2,0,1:T(8,128)(2,1)}, u32[]{:S(2)}) copy-start(bf16[512,1,1024]{2,0,1:T(8,128)(2,1)} %reduce-scatter.29.cloned.1.call-done) | copy-start | bytes 3145732
  (8 other events, 10.5 us)
Sparse Core Ops, SparseCore 0:
  10.2 64.6 all-gather.14
  77.1 44.0 all-gather.18
  123.4 31.9 all-gather.16
  157.3 37.9 all-gather.20
  199.8 30.7 reduce-scatter.22
  232.8 50.5 all-gather.24
  285.6 31.5 all-gather.22
  319.6 50.5 all-gather.26
  371.8 31.5 all-gather.28
  425.1 31.8 reduce-scatter.26
  459.2 31.8 reduce-scatter.24
  498.6 33.1 all-gather.30
  633.7 31.8 reduce-scatter.28
  668.7 9.8 reduce-scatter.30
  682.2 72.8 reduce-scatter.40
  759.3 71.4 reduce-scatter.38
  834.1 54.0 reduce-scatter.48
  892.1 54.0 reduce-scatter.46
  949.9 56.3 reduce-scatter.36
  1009.0 13.6 reduce-scatter.42
  1026.7 55.0 reduce-scatter.44
  1085.6 65.1 reduce-scatter.34
  1154.7 84.1 reduce-scatter.32
where the time goes:
time: 1250 us
  waiting for transfers between devices  822 us (66%)
  matrix products  171 us (14%)
  blocking collectives  120 us (10%)
  other arithmetic  79.5 us (6%)
  local copies, waits for them, and re-layouts  38.3 us (3%)
  between operations  15.5 us (1%)
    unnamed x27, waiting for transfers between devices  185 us
    reduce_scatter x1, waiting for transfers between devices, local(): lax.psum_scatter(mod_grad.astype(jnp.bfloat16), 'dp', scatter_dimension=0...  86.4 us
    reduce_scatter x1, waiting for transfers between devices, local(): lax.psum_scatter(up_grad.astype(jnp.bfloat16), 'dp', scatter_dimension=0,...  70.3 us
    reduce_scatter x1, waiting for transfers between devices, local(): lax.psum_scatter(qkv_grad.astype(jnp.bfloat16), 'dp', scatter_dimension=0...  67.6 us
    reduce_scatter x1, waiting for transfers between devices, local(): lax.psum_scatter(out_grad.astype(jnp.bfloat16), 'dp', scatter_dimension=1...  58.7 us
    all_gather x1, waiting for transfers between devices, local(): lax.all_gather(down_projection_weight, 'dp', axis=1, tiled=True)  42.5 us
    all_gather x1, waiting for transfers between devices, local(): lax.all_gather(modulation_weight, 'dp', axis=0, tiled=True)  39.4 us
    all_gather x1, waiting for transfers between devices, local(): input_m_full = lax.all_gather(input_m, 'mp', axis=0, tiled=True)  33.8 us
  transfers between devices with their start and end apart: 23, of which 20 were waited for; matrix products, arithmetic and copies ran while one was open for 12% of the time, Pallas kernels for 0%

commit v1 on v0

v1 whole, which is shorter than its diff:
```python
import jax
import jax.numpy as jnp
from jax import lax
from jax.experimental import pallas as pl
from jax.experimental.pallas import tpu as pltpu
from jax.sharding import PartitionSpec as P

HEAD_DIM = 64
PAIR = 2 * HEAD_DIM
TEMPER = HEAD_DIM ** (-0.5)

epsilon = 1e-06
precise = lax.Precision.HIGHEST
f32 = jnp.float32
bf16 = jnp.bfloat16


def layer_norm(values):
    center = values - jnp.mean(values, axis=-1, keepdims=True)
    inverse = lax.rsqrt(jnp.mean(center * center, axis=-1, keepdims=True) + epsilon)
    return (center * inverse, inverse)


def norm_back(grad_normed, normed, inverse):
    first = jnp.mean(grad_normed, axis=-1, keepdims=True)
    second = jnp.mean(grad_normed * normed, axis=-1, keepdims=True)
    return inverse * (grad_normed - first - normed * second)


def gelu_tanh(values):
    return jax.nn.gelu(values, approximate=True)


def dot(a, b, contract):
    return lax.dot_general(a, b, (contract, ((), ())), preferred_element_type=f32)


def nn(a, b):
    return dot(a, b, ((1,), (0,)))


def nt(a, b):
    return dot(a, b, ((1,), (1,)))


def tn(a, b):
    return dot(a, b, ((0,), (0,)))


def head_columns(ref, part, head, rows=slice(None)):
    start = part * PAIR + head * HEAD_DIM
    return ref[rows, start : start + HEAD_DIM]


def softmax_columns(scores):
    exponent = jnp.exp(scores - jnp.max(scores, axis=0, keepdims=True))
    return exponent * (1.0 / jnp.sum(exponent, axis=0, keepdims=True))


def attend_kernel(block, qkv_ref, out_ref):
    keys = [head_columns(qkv_ref, 1, h) for h in range(2)]
    values_t = [head_columns(qkv_ref, 2, h).T for h in range(2)]
    for first in range(0, qkv_ref.shape[0], block):
        rows = slice(first, first + block)
        parts = []
        for h in range(2):
            query = head_columns(qkv_ref, 0, h, rows) * TEMPER
            probs = softmax_columns(nt(keys[h], query)).astype(bf16)
            parts.append(nn(values_t[h], probs))
        out_ref[rows, :] = jnp.concatenate(parts, axis=0).T.astype(bf16)


def attend_back_kernel(block, qkv_ref, grad_ref, out_ref, grad_key, grad_value):
    keys = [head_columns(qkv_ref, 1, h) for h in range(2)]
    values = [head_columns(qkv_ref, 2, h) for h in range(2)]
    keys_t = [keys[h].T for h in range(2)]
    for first in range(0, qkv_ref.shape[0], block):
        rows = slice(first, first + block)
        parts = []
        for h in range(2):
            query = head_columns(qkv_ref, 0, h, rows) * TEMPER
            grad = grad_ref[rows, h * HEAD_DIM : (h + 1) * HEAD_DIM]
            probs = softmax_columns(nt(keys[h], query))
            grad_probs = nt(values[h], grad)
            inner = jnp.sum(probs * grad_probs, axis=0, keepdims=True)
            grad_scores = (probs * (grad_probs - inner)).astype(bf16)
            value_part = nn(probs.astype(bf16), grad)
            key_part = nn(grad_scores, query)
            if first == 0:
                grad_value[h] = value_part
                grad_key[h] = key_part
            else:
                grad_value[h] += value_part
                grad_key[h] += key_part
            parts.append(nn(keys_t[h], grad_scores))
        out_ref[rows, :PAIR] = (jnp.concatenate(parts, axis=0).T * TEMPER).astype(bf16)
    out_ref[:, PAIR : 2 * PAIR] = jnp.concatenate([grad_key[0], grad_key[1]], axis=1).astype(bf16)
    out_ref[:, 2 * PAIR :] = jnp.concatenate([grad_value[0], grad_value[1]], axis=1).astype(bf16)


def attend(qkv):
    tokens, width = qkv.shape
    pairs = width // (3 * PAIR)
    block = min(256, tokens)

    def body(qkv_ref, out_ref):
        attend_kernel(block, qkv_ref, out_ref)

    return pl.pallas_call(
        body,
        grid=(pairs,),
        in_specs=[pl.BlockSpec((tokens, 3 * PAIR), lambda p: (0, p))],
        out_specs=pl.BlockSpec((tokens, PAIR), lambda p: (0, p)),
        out_shape=jax.ShapeDtypeStruct((tokens, pairs * PAIR), bf16),
        compiler_params=pltpu.CompilerParams(vmem_limit_bytes=40 * 2**20),
        cost_estimate=pl.CostEstimate(
            flops=16 * pairs * tokens * tokens * PAIR,
            bytes_accessed=8 * tokens * pairs * PAIR,
            transcendentals=2 * pairs * tokens * tokens,
        ),
        name="attend",
    )(qkv)


def attend_back(qkv, grad):
    tokens, width = qkv.shape
    pairs = width // (3 * PAIR)
    block = min(256, tokens)

    def body(*refs):
        attend_back_kernel(block, *refs)

    return pl.pallas_call(
        body,
        grid=(pairs,),
        in_specs=[
            pl.BlockSpec((tokens, 3 * PAIR), lambda p: (0, p)),
            pl.BlockSpec((tokens, PAIR), lambda p: (0, p)),
        ],
        out_specs=pl.BlockSpec((tokens, 3 * PAIR), lambda p: (0, p)),
        out_shape=jax.ShapeDtypeStruct((tokens, width), bf16),
        scratch_shapes=[
            pltpu.VMEM((2, tokens, HEAD_DIM), f32),
            pltpu.VMEM((2, tokens, HEAD_DIM), f32),
        ],
        compiler_params=pltpu.CompilerParams(vmem_limit_bytes=40 * 2**20),
        cost_estimate=pl.CostEstimate(
            flops=40 * pairs * tokens * tokens * PAIR,
            bytes_accessed=14 * tokens * pairs * PAIR,
            transcendentals=2 * pairs * tokens * tokens,
        ),
        name="attend_back",
    )(qkv, grad)


def by_pairs(matrix):
    rows, parts, width = matrix.shape
    split = matrix.reshape(rows, parts, width // PAIR, PAIR)
    return jnp.swapaxes(split, 1, 2).reshape(rows, parts * width)


def from_pairs(matrix):
    rows, width = matrix.shape
    split = matrix.reshape(rows, width // (3 * PAIR), 3, PAIR)
    return jnp.swapaxes(split, 1, 2).reshape(rows, 3, width // 3)


def swap(values):
    return lax.ppermute(values, "mp", [(0, 1), (1, 0)])


def expand(values):
    if lax.axis_size("mp") == 2:
        return [values, swap(values)]
    return [lax.all_gather(values, "mp", axis=0, tiled=True)]


def owned_sums(function, chunks):
    if lax.axis_size("mp") == 2:
        received = swap(function(chunks[1]).astype(bf16))
        return function(chunks[0]) + received.astype(f32)
    return lax.psum_scatter(
        function(chunks[0]).astype(bf16), "mp", scatter_dimension=0, tiled=True
    ).astype(f32)


def chunked(values, count):
    return jnp.split(values, count, axis=0) if count > 1 else [values]


def joined(chunks):
    return jnp.concatenate(chunks, axis=0) if len(chunks) > 1 else chunks[0]


def to_latents(values):
    dp, mp = lax.axis_size("dp"), lax.axis_size("mp")
    width = values.shape[1]
    repeated = jnp.broadcast_to(values[:, None], (dp, mp, width)).reshape(dp * mp, width)
    received = lax.all_to_all(repeated, ("dp", "mp"), 0, 0, tiled=True)
    return received.reshape(dp, mp, width)


def local(
    latents,
    condition,
    modulation_weight,
    modulation_bias,
    query_key_value_weight,
    query_value_bias,
    attention_output_weight,
    up_projection_weight,
    up_projection_bias,
    down_projection_weight,
    projection_row_bias,
    cotangent,
):
    mp, dp = lax.axis_size("mp"), lax.axis_size("dp")
    my_dp, my_mp = lax.axis_index("dp"), lax.axis_index("mp")
    model_width = latents.shape[2]
    width = model_width // mp
    rows = model_width // dp
    ff = up_projection_weight.shape[1]
    tokens_in = latents[0].astype(f32)
    grad_out = cotangent[0].astype(f32)
    cond_float = condition.astype(f32)
    activated = jax.nn.silu(cond_float).astype(bf16)

    small_parts = [
        activated,
        modulation_bias.reshape(1, -1),
        query_value_bias.reshape(1, -1),
        up_projection_bias.reshape(1, -1),
        projection_row_bias.reshape(1, -1),
    ]
    bounds = []
    for part in small_parts:
        start = bounds[-1][1] if bounds else 0
        bounds.append((start, start + part.shape[1]))
    small = lax.all_gather(jnp.concatenate(small_parts, axis=1), "dp", axis=0, tiled=True)
    small_out = [small[:, a:b] for a, b in bounds]

    def bias_rows(gathered, count):
        split = gathered.reshape(dp, count, -1)
        return jnp.swapaxes(split, 0, 1).reshape(count, -1).astype(f32)

    mod_offset = bias_rows(small_out[1], 6)
    qv_offset = bias_rows(small_out[2], 2)
    up_offset = bias_rows(small_out[3], 1)
    row_offset = bias_rows(small_out[4], 2)
    act_rows = lax.dynamic_slice_in_dim(small_out[0], my_dp * rows, rows, axis=1)

    qkv_matrix = lax.all_gather(by_pairs(query_key_value_weight), "dp", axis=0, tiled=True)
    packed = jnp.concatenate(
        [attention_output_weight.T, up_projection_weight, down_projection_weight.T], axis=1
    )
    packed_full = lax.all_gather(packed, "dp", axis=0, tiled=True)
    out_matrix_t = packed_full[:, :width]
    up_matrix = packed_full[:, width : width + ff]
    down_matrix_t = packed_full[:, width + ff :]

    mod_flat = modulation_weight.reshape(rows, -1)
    mod_partial = nn(act_rows, mod_flat)
    extra = jnp.concatenate([mod_offset.reshape(1, -1), row_offset.reshape(1, -1)], axis=1)
    payload = jnp.pad(mod_partial, ((0, 0), (0, 2 * width))) + jnp.where(my_dp == 0, extra, 0.0)
    arrived = jnp.sum(to_latents(payload), axis=0).reshape(mp, 8, width)
    vectors = jnp.swapaxes(arrived, 0, 1).reshape(8, 1, model_width)
    shift_attn, scale_attn, gate_attn, shift_mlp, scale_mlp, gate_mlp = (
        vectors[k] for k in range(6)
    )

    normed_a, inverse_a = layer_norm(tokens_in)
    input_a = (normed_a * (1.0 + scale_attn) + shift_attn).astype(bf16)
    chunks_a = expand(input_a)
    count = len(chunks_a)
    qkv_shift = by_pairs(jnp.stack([qv_offset[0], jnp.zeros_like(qv_offset[0]), qv_offset[1]])[None])
    qkv = joined([(nn(chunk, qkv_matrix) + qkv_shift).astype(bf16) for chunk in chunks_a])
    grad_branch_mlp = (gate_mlp * grad_out).astype(bf16)
    chunks_grad_mlp = expand(grad_branch_mlp)

    attended = attend(qkv)
    branch_attn = (
        owned_sums(lambda chunk: nt(chunk, out_matrix_t), chunked(attended, count)) + vectors[6]
    )
    middle = tokens_in + gate_attn * branch_attn
    normed_m, inverse_m = layer_norm(middle)
    input_m = (normed_m * (1.0 + scale_mlp) + shift_mlp).astype(bf16)
    chunks_m = expand(input_m)
    pre_up = [nn(chunk, up_matrix) + up_offset for chunk in chunks_m]
    hidden = [gelu_tanh(chunk).astype(bf16) for chunk in pre_up]

    grad_pre_up = []
    for grad_chunk, pre_chunk in zip(chunks_grad_mlp, pre_up):
        unused_gelu, gelu_back = jax.vjp(gelu_tanh, pre_chunk)
        grad_pre_up.append(gelu_back(nn(grad_chunk, down_matrix_t))[0].astype(bf16))
    grad_input_m = owned_sums(lambda chunk: nt(chunk, up_matrix), grad_pre_up)
    branch_mlp = owned_sums(lambda chunk: nt(chunk, down_matrix_t), hidden) + vectors[7]
    result_out = middle + gate_mlp * branch_mlp
    grad_gate_mlp = jnp.sum(grad_out * branch_mlp, axis=0)
    grad_pre_full = joined(grad_pre_up)
    up_grad = tn(joined(chunks_m), grad_pre_full).astype(bf16)
    down_grad_t = tn(joined(chunks_grad_mlp), joined(hidden)).astype(bf16)
    up_bias_part = jnp.sum(grad_pre_full, axis=0, dtype=f32)
    mlp_grads = lax.psum_scatter(
        jnp.concatenate([up_grad, down_grad_t], axis=1), "dp", scatter_dimension=0, tiled=True
    ).astype(f32)

    grad_shift_mlp = jnp.sum(grad_input_m, axis=0)
    grad_scale_mlp = jnp.sum(grad_input_m * normed_m, axis=0)
    grad_middle = grad_out + norm_back(grad_input_m * (1.0 + scale_mlp), normed_m, inverse_m)
    grad_gate_attn = jnp.sum(grad_middle * branch_attn, axis=0)
    grad_branch_attn = (gate_attn * grad_middle).astype(bf16)
    chunks_grad_attn = expand(grad_branch_attn)
    grad_attended = joined([nn(chunk, out_matrix_t).astype(bf16) for chunk in chunks_grad_attn])
    grad_qkv = attend_back(qkv, grad_attended)
    out_grad_t = tn(joined(chunks_grad_attn), attended).astype(bf16)
    grad_input_a = owned_sums(lambda chunk: nt(chunk, qkv_matrix), chunked(grad_qkv, count))
    qkv_grad = tn(joined(chunks_a), grad_qkv).astype(bf16)
    attn_grads = lax.psum_scatter(
        jnp.concatenate([qkv_grad, out_grad_t], axis=1), "dp", scatter_dimension=0, tiled=True
    ).astype(f32)
    qkv_bias_part = from_pairs(jnp.sum(grad_qkv, axis=0, dtype=f32)[None])[0]
    grad_shift_attn = jnp.sum(grad_input_a, axis=0)
    grad_scale_attn = jnp.sum(grad_input_a * normed_a, axis=0)
    grad_tokens = grad_middle + norm_back(grad_input_a * (1.0 + scale_attn), normed_a, inverse_a)

    token_sums = jnp.stack(
        [
            grad_shift_attn,
            grad_scale_attn,
            grad_gate_attn,
            grad_shift_mlp,
            grad_scale_mlp,
            grad_gate_mlp,
            jnp.sum(grad_branch_attn, axis=0, dtype=f32),
            jnp.sum(grad_branch_mlp, axis=0, dtype=f32),
        ]
    )
    if mp == 2:
        own = lax.dynamic_slice_in_dim(token_sums, my_mp * width, width, axis=1)
        other = lax.dynamic_slice_in_dim(token_sums, (1 - my_mp) * width, width, axis=1)
        column_sums = own + swap(other)
    else:
        column_sums = lax.psum_scatter(token_sums, "mp", scatter_dimension=1, tiled=True)
    mine = jnp.concatenate(
        [column_sums.reshape(1, -1), qkv_bias_part[0:1], qkv_bias_part[2:3], up_bias_part[None]],
        axis=1,
    )
    everyone = lax.all_gather(mine, "dp", axis=0, tiled=True)
    grad_mod_all = everyone[:, : 6 * width]
    sums = jnp.sum(everyone, axis=0)
    mod_grad = lax.dot_general(
        act_rows.astype(f32), grad_mod_all, (((0,), (0,)), ((), ())), precision=precise
    ).reshape(modulation_weight.shape)
    cond_partial = lax.dot_general(
        grad_mod_all, mod_flat.astype(f32), (((1,), (1,)), ((), ())), precision=precise
    )
    grad_activated = jnp.sum(to_latents(cond_partial), axis=1).reshape(1, model_width)
    unused_silu, silu_back = jax.vjp(jax.nn.silu, cond_float)
    cond_grad = lax.dynamic_slice_in_dim(
        silu_back(grad_activated)[0], my_mp * width, width, axis=1
    )

    share = width // dp
    column_totals = sums[: 10 * width].reshape(10, width)
    column_share = lax.dynamic_slice_in_dim(column_totals, my_dp * share, share, axis=1)
    up_share = lax.dynamic_slice_in_dim(sums[10 * width :], my_dp * (ff // dp), ff // dp)

    qkv_cols = 3 * width
    return (
        result_out.astype(bf16)[None],
        grad_tokens.astype(bf16)[None],
        cond_grad.astype(bf16),
        mod_grad,
        column_share[:6],
        from_pairs(attn_grads[:, :qkv_cols]),
        column_share[8:10],
        attn_grads[:, qkv_cols:].T,
        mlp_grads[:, :ff],
        up_share,
        mlp_grads[:, ff:].T,
        column_share[6:8],
    )


def solution(mesh):
    placed = (
        P("dp", "mp", None),
        P("dp", None),
        P("dp", None, "mp"),
        P(None, ("mp", "dp")),
        P("dp", None, "mp"),
        P(None, ("mp", "dp")),
        P("mp", "dp"),
        P("dp", "mp"),
        P(("mp", "dp")),
        P("mp", "dp"),
        P(None, ("mp", "dp")),
        P("dp", "mp", None),
    )
    return jax.shard_map(
        local,
        mesh=mesh,
        in_specs=placed,
        out_specs=(
            P("dp", "mp", None),
            P("dp", "mp", None),
            P("dp", "mp"),
            P("dp", None, "mp"),
            P(None, ("mp", "dp")),
            P("dp", None, "mp"),
            P(None, ("mp", "dp")),
            P("mp", "dp"),
            P("dp", "mp"),
            P(("mp", "dp")),
            P("mp", "dp"),
            P(None, ("mp", "dp")),
        ),
        check_vma=False,
    )
```

time: 1250 us -> 561 us (0.45)
  waiting for transfers between devices: 822 us -> 285 us
  matrix products: 171 us -> 80.1 us
  blocking collectives: 120 us -> 43.2 us
  Pallas kernels: 0 us -> 66.9 us
  other arithmetic: 79.5 us -> 28.1 us
  local copies, waits for them, and re-layouts: 38.3 us -> 19.5 us
  starting transfers between devices: 1.79 us -> 17.2 us
    reduce_scatter x10 -> x2, waiting for transfers between devices: 396 us -> 78.4 us  [the longest x1 78.4 us: local(): lax.psum_scatter(jnp.concatenate([up_grad, down_grad_t], axis=1), 'dp', s...]
    all_gather x9 -> x2, waiting for transfers between devices: 241 us -> 25.5 us  [the longest x1 25.5 us: local(): packed_full = lax.all_gather(packed, 'dp', axis=0, tiled=True)]
    unnamed x27 -> x4, waiting for transfers between devices: 185 us -> 0.07 us
    ppermute x0 -> x9, waiting for transfers between devices: none -> 153 us  [swap(): return lax.ppermute(values, 'mp', [(0, 1), (1, 0)])]
    dot_general x28 -> x23, matrix products: 171 us -> 80.1 us  [the longest x21 78.4 us: dot(): lax.dot_general(a, b, (contract, ((), ())), preferred_element_type=f32)]
    pallas_call x0 -> x2, Pallas kernels: none -> 66.9 us  [the longest x1 39.9 us: attend_back(): pl.pallas_call(body, grid=(pairs,), in_specs=[pl.BlockSpec((tokens, 3 * P...]
    convert_element_type x23 -> x9, other arithmetic: 46.7 us -> 3.3 us  [the longest x1 1.11 us: local(): mlp_grads = lax.psum_scatter(jnp.concatenate([up_grad, down_grad_t], axis...]
    all_gather x5 -> x2, blocking collectives: 86.2 us -> 43.2 us  [the longest x1 23.5 us: local(): lax.all_gather(jnp.concatenate(small_parts, axis=1), 'dp', axis=0, tiled=...]
  transfers between devices with their start and end apart: 23 -> 15, of which waited for: 20 -> 12; matrix products, arithmetic and copies ran while one was open for 12% -> 16% of each run, Pallas kernels for 0% -> 5%
where the time goes in v1:
time: 561 us; the launch traced here: 555 us
  waiting for transfers between devices  285 us (51%)
  matrix products  80.1 us (14%)
  Pallas kernels  66.9 us (12%)
  blocking collectives  43.2 us (8%)
  other arithmetic  28.1 us (5%)
  local copies, waits for them, and re-layouts  19.5 us (3%)
  starting transfers between devices  17.2 us (3%)
  between operations  14.9 us (3%)
    ppermute x9, waiting for transfers between devices, swap(): return lax.ppermute(values, 'mp', [(0, 1), (1, 0)])  153 us
    dot_general x21, matrix products, dot(): lax.dot_general(a, b, (contract, ((), ())), preferred_element_type=f32)  78.4 us
    reduce_scatter x1, waiting for transfers between devices, local(): lax.psum_scatter(jnp.concatenate([up_grad, down_grad_t], axis=1), 'dp', s...  78.4 us
    pallas_call x1, Pallas kernels, attend_back(): pl.pallas_call(body, grid=(pairs,), in_specs=[pl.BlockSpec((tokens, 3 * P...  39.9 us
    all_to_all x2, waiting for transfers between devices, to_latents(): received = lax.all_to_all(repeated, ('dp', 'mp'), 0, 0, tiled=True)  27.7 us
    pallas_call x1, Pallas kernels, attend(): pl.pallas_call(body, grid=(pairs,), in_specs=[pl.BlockSpec((tokens, 3 * P...  27 us
    all_gather x1, waiting for transfers between devices, local(): packed_full = lax.all_gather(packed, 'dp', axis=0, tiled=True)  25.5 us
    all_gather x1, blocking collectives, local(): lax.all_gather(jnp.concatenate(small_parts, axis=1), 'dp', axis=0, tiled=...  23.5 us
  transfers between devices with their start and end apart: 15, of which 12 were waited for; matrix products, arithmetic and copies ran while one was open for 16% of the time, Pallas kernels for 5%

profile of v1, /device:TPU:0, one launch (start us, length us, event | category | flops | bytes accessed | tf_op | source)
XLA Modules:
  0.0 554.5 jit_solution(4447692990188561388)
XLA Ops:
  7.3 1.0 reshape.237
  8.5 0.8 reshape.238
  9.4 1.9 pad_maximum_fusion.6
  12.3 23.5 %all-gather = bf16[16,1,1472]{2,1,0:T(2,128)(2,1)S(1)} all-gather(bf16[1,1,1472]{2,1,0:T(2,128)(2,1)S(1)} %bitcast.185), channel_id=1, replica_groups=mesh['dp'=16,'mp'=2] {'dp'}, dimensions={0}, use_global_device_ids=true | all-gather | bytes 50048 | tf_op jit(solution)/shard_map/all_gather | solution.py:239
  37.0 1.6 all_to_all.12
  38.6 2.6 all-to-all-start
  41.9 24.7 %all-to-all-done = f32[32,1,4096]{2,1,0:T(1,128)S(1)} async-done(((f32[32,1,4096]{2,1,0:T(1,128)}), f32[32,1,4096]{2,1,0:T(1,128)S(1)}, u32[]{:S(2)}, u32[]{:S(2)}) %all-to-all-start) | async-done | bytes 524320 | tf_op jit(solution)/shard_map/all_to_all | solution.py:199
  66.6 1.2 reduce.2
  68.9 1.5 collective-permute-start
  70.9 3.8 fusion.21
  74.7 19.9 %collective-permute-done = bf16[512,1024]{1,0:T(8,128)(2,1)} collective-permute-done((bf16[512,1024]{1,0:T(8,128)(2,1)S(1)}, bf16[512,1024]{1,0:T(8,128)(2,1)}, u32[]{:S(2)}, u32[]{:S(2)}) %collective-permute-start) | collective-permute-done | bytes 1048608 | tf_op jit(solution)/shard_map/ppermute | solution.py:169
  94.6 3.0 fusion.22
  97.8 27.0 %attend.1 = bf16[1024,512]{1,0:T(8,128)(2,1)S(1)} custom-call(bf16[1024,1536]{1,0:T(8,128)(2,1)S(1)} %pad_maximum_fusion.3.qkv_ref.refs_0_), custom_call_target="tpu_custom_call" | custom-call | flops 8589934592 | bytes 4194304 | tf_op jit(solution)/shard_map/attend/pallas_call | solution.py:109
  124.9 1.0 copy-done.2
  125.8 25.5 %all-gather.7.cloned.1.call-done = bf16[1024,4608]{1,0:T(8,128)(2,1)} async-done(((bf16[64,4608]{1,0:T(8,128)(2,1)}), bf16[1024,4608]{1,0:T(8,128)(2,1)}) %all-gather.7.cloned.1.call-update) | async-done | bytes 9437200 | tf_op jit(solution)/shard_map/all_gather | solution.py:256
  151.4 2.3 convolution_convert_fusion.2
  153.6 1.5 collective-permute-start.1
  156.2 23.5 %collective-permute-done.1 = bf16[512,1024]{1,0:T(8,128)(2,1)S(1)} collective-permute-done((bf16[512,1024]{1,0:T(8,128)(2,1)S(1)}, bf16[512,1024]{1,0:T(8,128)(2,1)S(1)}, u32[]{:S(2)}, u32[]{:S(2)}) %collective-permute-start.1) | collective-permute-done | bytes 1048608 | tf_op jit(solution)/shard_map/ppermute | solution.py:169
  179.7 3.9 fusion.121
  184.4 1.5 collective-permute-start.2
  185.9 2.3 fusion.37
  188.3 4.7 fusion.6
  193.0 31.0 %collective-permute-done.2 = bf16[512,1024]{1,0:T(8,128)(2,1)S(1)} collective-permute-done((bf16[512,1024]{1,0:T(8,128)(2,1)S(1)}, bf16[512,1024]{1,0:T(8,128)(2,1)S(1)}, u32[]{:S(2)}, u32[]{:S(2)}) %collective-permute-start.2) | collective-permute-done | bytes 1048608 | tf_op jit(solution)/shard_map/ppermute | solution.py:169
  224.0 6.4 %multiply_convert_fusion = (bf16[512,2048]{1,0:T(8,128)(2,1)S(1)}, bf16[512,2048]{1,0:T(8,128)(2,1)S(1)}, f32[512,2048]{1,0:T(8,128)}) fusion(f32[2048]{0:T(1024)S(1)} %fusion.106, f32[512,2048]{1,0:T(8,128)S(1)} %fusion.37, bf16[512,1024]{1,0:T(8,128)(2,1)S(1)} %collective-permute-done.2, bf16[1024,4608]{1,0:T(8,128)(2,1)S(1)} %copy-done.26), kind=kOutput, calls=%fused_computation.27 | convolution fusion | flops 2168455168 | bytes 17833984 | tf_op jit(solution)/shard_map/dot_general | solution.py:35
  230.3 7.8 %fusion.13 = bf16[512,2048]{1,0:T(8,128)(2,1)S(1)} fusion(f32[512,2048]{1,0:T(8,128)} %get-tuple-element.103, f32[2048]{0:T(1024)S(1)} %fusion.106, bf16[512,1024]{1,0:T(8,128)(2,1)S(1)} %collective-permute-done.4, bf16[1024,4608]{1,0:T(8,128)(2,1)S(1)} %copy-done.26), kind=kOutput, calls=%fused_computation.20 | convolution fusion | flops 2169503744 | bytes 11542528 | tf_op jit(solution)/shard_map/dot_general | solution.py:35
  238.1 2.4 fusion.87
  240.6 1.5 collective-permute-start.5
  242.1 2.4 fusion.90
  245.1 2.4 fusion.29
  247.5 19.3 %collective-permute-done.5 = bf16[512,1024]{1,0:T(8,128)(2,1)S(1)} collective-permute-done((bf16[512,1024]{1,0:T(8,128)(2,1)S(1)}, bf16[512,1024]{1,0:T(8,128)(2,1)S(1)}, u32[]{:S(2)}, u32[]{:S(2)}) %collective-permute-start.5) | collective-permute-done | bytes 1048608 | tf_op jit(solution)/shard_map/ppermute | solution.py:169
  266.8 3.0 multiply_reduce_fusion
  269.8 17.9 %collective-permute-done.3 = bf16[512,1024]{1,0:T(8,128)(2,1)S(1)} collective-permute-done((bf16[512,1024]{1,0:T(8,128)(2,1)S(1)}, bf16[512,1024]{1,0:T(8,128)(2,1)S(1)}, u32[]{:S(2)}, u32[]{:S(2)}) %collective-permute-start.3) | collective-permute-done | bytes 1048608 | tf_op jit(solution)/shard_map/ppermute | solution.py:169
  287.6 3.4 fusion.57
  291.0 1.5 collective-permute-start.6
  293.2 21.4 %collective-permute-done.6 = bf16[512,1024]{1,0:T(8,128)(2,1)S(1)} collective-permute-done((bf16[512,1024]{1,0:T(8,128)(2,1)S(1)}, bf16[512,1024]{1,0:T(8,128)(2,1)S(1)}, u32[]{:S(2)}, u32[]{:S(2)}) %collective-permute-start.6) | collective-permute-done | bytes 1048608 | tf_op jit(solution)/shard_map/ppermute | solution.py:169
  314.6 0.7 convolution_convert_fusion.3
  315.4 39.9 %attend_back.1 = bf16[1024,1536]{1,0:T(8,128)(2,1)S(1)} custom-call(bf16[1024,1536]{1,0:T(8,128)(2,1)S(1)} %pad_maximum_fusion.3.qkv_ref.refs_0_, bf16[1024,512]{1,0:T(8,128)(2,1)S(1)} %pad_maximum_fusion.5.refs_1_), custom_call_target="tpu_custom_call" | custom-call | flops 21474836480 | bytes 7340032 | tf_op jit(solution)/shard_map/attend_back/pallas_call | solution.py:133
  355.3 1.3 fusion.84
  357.3 5.0 convolution_convert_fusion
  362.3 2.6 pad_maximum_fusion.2
  365.0 1.1 copy-done.22
  366.2 9.3 %fusion.18 = bf16[1024,2048]{1,0:T(8,128)(2,1)} fusion(bf16[512,2048]{1,0:T(8,128)(2,1)} %copy-done.39, bf16[512,2048]{1,0:T(8,128)(2,1)} %copy-done.38, bf16[512,1024]{1,0:T(8,128)(2,1)} %copy-done.33, bf16[512,1024]{1,0:T(8,128)(2,1)S(1)} %copy-done.22), kind=kOutput, calls=%fused_computation.29 | convolution fusion | flops 4309647360 | bytes 10485760 | tf_op jit(solution)/shard_map/dot_general | solution.py:35
  375.5 6.6 %convolution_convert_fusion.1 = bf16[1024,2048]{1,0:T(8,128)(2,1)} fusion(bf16[512,2048]{1,0:T(8,128)(2,1)S(1)} %copy-done.17, bf16[512,2048]{1,0:T(8,128)(2,1)S(1)} %copy-done.15, bf16[512,1024]{1,0:T(8,128)(2,1)S(1)} %copy-done.35, bf16[512,1024]{1,0:T(8,128)(2,1)S(1)} %copy-done.24), kind=kOutput, calls=%fused_computation.31 | convolution fusion | flops 4309647360 | bytes 10485760 | tf_op jit(solution)/shard_map/dot_general | solution.py:35
  382.1 8.0 %pad_maximum_fusion = bf16[1024,4096]{1,0:T(8,128)(2,1)} fusion(bf16[1024,2048]{1,0:T(8,128)(2,1)} %fusion.18, bf16[1024,2048]{1,0:T(8,128)(2,1)} %convolution_convert_fusion.1), kind=kLoop, calls=%fused_computation | loop fusion | flops 16777216 | bytes 16777216 | tf_op jit(solution)/shard_map/concatenate | solution.py:304
  390.0 1.9 copy-done.1
  391.9 5.2 fusion.81
  397.1 1.4 collective-permute-start.7
  398.5 2.9 convert_reduce_fusion
  402.0 17.8 %collective-permute-done.7 = bf16[512,1024]{1,0:T(8,128)(2,1)} collective-permute-done((bf16[512,1024]{1,0:T(8,128)(2,1)}, bf16[512,1024]{1,0:T(8,128)(2,1)}, u32[]{:S(2)}, u32[]{:S(2)}) %collective-permute-start.7) | collective-permute-done | bytes 1048608 | tf_op jit(solution)/shard_map/ppermute | solution.py:169
  419.7 5.1 fusion.54
  424.9 2.1 multiply_reduce_fusion.1
  427.0 1.5 collective-permute-start.8
  428.6 2.3 collective-permute-done.8
  430.9 19.7 %all-gather.1 = f32[16,1,7168]{2,1,0:T(1,128)S(1)} all-gather(f32[1,1,7168]{2,1,0:T(1,128)S(1)} %maximum_bitcast_fusion), channel_id=1, replica_groups=mesh['dp'=16,'mp'=2] {'dp'}, dimensions={0}, use_global_device_ids=true | all-gather | bytes 487424 | tf_op jit(solution)/shard_map/all_gather | solution.py:348
  452.0 2.6 all-to-all-start.1
  455.3 1.3 fusion.102
  457.2 0.9 copy.61
  458.7 3.0 all-to-all-done.1
  462.4 1.0 slice.177
  463.8 0.9 reshape.244
  465.5 78.4 %reduce-scatter.5.cloned.1.call-done = bf16[64,4096]{1,0:T(8,128)(2,1)} async-done(((bf16[1024,4096]{1,0:T(8,128)(2,1)}), bf16[64,4096]{1,0:T(8,128)(2,1)}) %reduce-scatter.5.cloned.1.call-update) | async-done | bytes 524304 | tf_op jit(solution)/shard_map/reduce_scatter | solution.py:303
  543.8 1.1 convert_element_type.219
  544.9 0.8 slice_bitcast_fusion
  545.8 1.8 slice.179
  (165 shorter events, 14.4 us)
Async XLA Ops:
  7.2 4.2 copy-start.30
  7.2 4.3 copy-start.36
  7.2 4.3 copy-start.37
  7.2 4.4 copy-start.28
  7.2 5.0 copy-start.31
  7.2 28.7 %copy-start.25 = (bf16[64,6,512]{2,0,1:T(8,128)(2,1)S(1)}, bf16[64,6,512]{2,0,1:T(8,128)(2,1)}, u32[]{:S(2)}) copy-start(bf16[64,6,512]{2,0,1:T(8,128)(2,1)} %param.14) | copy-start | bytes 1179652
  7.2 63.6 %all-gather.5.cloned.1.call-start = ((), (), s32[]{:S(2)}) async-start(), calls=%async_computation.4 | async-start | bytes 3342336 | tf_op jit(solution)/shard_map/all_gather | solution.py:252
  9.4 142.0 %all-gather.7.cloned.1.call-start = ((), (), s32[]{:S(2)}) async-start(), calls=%async_computation.5 | async-start | bytes 10027008 | tf_op jit(solution)/shard_map/all_gather | solution.py:256
  11.3 30.0 %copy-start.4 = (bf16[1,512,1024]{2,1,0:T(8,128)(2,1)S(1)}, bf16[1,512,1024]{2,1,0:T(8,128)(2,1)}, u32[]{:S(2)}) copy-start(bf16[1,512,1024]{2,1,0:T(8,128)(2,1)} %param.12) | copy-start | bytes 3145732
  35.9 0.8 copy-start.27
  36.0 6.0 %copy-start.12 = (bf16[6,8,8,512]{3,2,0,1:T(8,128)(2,1)}, bf16[6,8,8,512]{3,2,0,1:T(8,128)(2,1)S(1)}, u32[]{:S(2)}) copy-start(bf16[6,8,8,512]{3,2,0,1:T(8,128)(2,1)S(1)} %copy.52) | copy-start | bytes 1179652
  38.6 28.0 %all-to-all-start = ((f32[32,1,4096]{2,1,0:T(1,128)}), f32[32,1,4096]{2,1,0:T(1,128)S(1)}, u32[]{:S(2)}, u32[]{:S(2)}) async-start(f32[32,1,4096]{2,1,0:T(1,128)} %all_to_all.12), calls=%async_computation | async-start | bytes 1048576 | tf_op jit(solution)/shard_map/all_to_all | solution.py:199
  41.2 421.2 %reduce-scatter.3.cloned.1.call-start = ((), (), s32[]{:S(2)}) async-start(), calls=%async_computation.6 | async-start | bytes 4456448 | tf_op jit(solution)/shard_map/reduce_scatter | solution.py:318
  68.9 5.8 %copy-start.19 = (bf16[512,1024]{1,0:T(8,128)(2,1)}, bf16[512,1024]{1,0:T(8,128)(2,1)S(1)}, u32[]{:S(2)}) copy-start(bf16[512,1024]{1,0:T(8,128)(2,1)S(1)} %fusion.48) | copy-start | bytes 3145732
  68.9 25.7 %collective-permute-start = (bf16[512,1024]{1,0:T(8,128)(2,1)S(1)}, bf16[512,1024]{1,0:T(8,128)(2,1)}, u32[]{:S(2)}, u32[]{:S(2)}) collective-permute-start(bf16[512,1024]{1,0:T(8,128)(2,1)S(1)} %fusion.48), channel_id=1, source_target_pairs={{0,1},{1,0},{2,3},{3,2},{4,5},{5,4},{6,7},{7,6},{8,9},{9,8},{10,11... | collective-permute-start | bytes 3145736 | tf_op jit(solution)/shard_map/ppermute | solution.py:169
  70.8 23.7 %copy-start.32 = (bf16[1024,1536]{1,0:T(8,128)(2,1)S(1)}, bf16[1024,1536]{1,0:T(8,128)(2,1)}, u32[]{:S(2)}) copy-start(bf16[1024,1536]{1,0:T(8,128)(2,1)} %all-gather.5.cloned.1.call-done) | copy-start | bytes 9437188
  124.9 1.0 copy-start.2
  151.3 3.8 copy-start.11
  151.3 28.3 %copy-start.3 = (bf16[1024,512]{1,0:T(8,128)(2,1)S(1)}, bf16[1024,512]{1,0:T(8,128)(2,1)}, u32[]{:S(2)}) copy-start(bf16[1024,512]{1,0:T(8,128)(2,1)} %copy-done.2) | copy-start | bytes 3145732
  151.4 28.3 %copy-start.5 = (bf16[1,512,1024]{2,1,0:T(8,128)(2,1)S(1)}, bf16[1,512,1024]{2,1,0:T(8,128)(2,1)}, u32[]{:S(2)}) copy-start(bf16[1,512,1024]{2,1,0:T(8,128)(2,1)} %param.12) | copy-start | bytes 3145732
  153.6 26.1 %collective-permute-start.1 = (bf16[512,1024]{1,0:T(8,128)(2,1)S(1)}, bf16[512,1024]{1,0:T(8,128)(2,1)S(1)}, u32[]{:S(2)}, u32[]{:S(2)}) collective-permute-start(bf16[512,1024]{1,0:T(8,128)(2,1)S(1)} %convolution_convert_fusion.2), channel_id=1, source_target_pairs={{0,1},{1,0},{2,3},{3,2},{4,5},{5,4},{6,7},{7,6},{8,9},{9,8},{10,11... | collective-permute-start | bytes 3145736 | tf_op jit(solution)/shard_map/ppermute | solution.py:169
  155.5 32.8 %copy-start.21 = (bf16[512,1024]{1,0:T(8,128)(2,1)}, bf16[512,1024]{1,0:T(8,128)(2,1)S(1)}, u32[]{:S(2)}) copy-start(bf16[512,1024]{1,0:T(8,128)(2,1)S(1)} %get-tuple-element.71) | copy-start | bytes 3145732
  155.5 74.8 %collective-permute-start.4 = (bf16[512,1024]{1,0:T(8,128)(2,1)S(1)}, bf16[512,1024]{1,0:T(8,128)(2,1)S(1)}, u32[]{:S(2)}, u32[]{:S(2)}) collective-permute-start(bf16[512,1024]{1,0:T(8,128)(2,1)S(1)} %get-tuple-element.71), channel_id=1, source_target_pairs={{0,1},{1,0},{2,3},{3,2},{4,5},{5,4},{6,7},{7,6},{8,9},{9,8},{10,11... | collective-permute-start | bytes 3145736 | tf_op jit(solution)/shard_map/ppermute | solution.py:169
  179.7 3.9 copy-start.9
  179.7 6.2 %copy-start.26 = (bf16[1024,4608]{1,0:T(8,128)(2,1)S(1)}, bf16[1024,4608]{1,0:T(8,128)(2,1)}, u32[]{:S(2)}) copy-start(bf16[1024,4608]{1,0:T(8,128)(2,1)} %all-gather.7.cloned.1.call-done) | copy-start | bytes 28311556
  184.4 3.9 copy-start.23
  184.4 39.6 %collective-permute-start.2 = (bf16[512,1024]{1,0:T(8,128)(2,1)S(1)}, bf16[512,1024]{1,0:T(8,128)(2,1)S(1)}, u32[]{:S(2)}, u32[]{:S(2)}) collective-permute-start(bf16[512,1024]{1,0:T(8,128)(2,1)S(1)} %add_convert_fusion.1), channel_id=1, source_target_pairs={{0,1},{1,0},{2,3},{3,2},{4,5},{5,4},{6,7},{7,6},{8,9},{9,8},{10,11... | collective-permute-start | bytes 3145736 | tf_op jit(solution)/shard_map/ppermute | solution.py:169
  193.0 73.8 %copy-start.14 = (bf16[512,2048]{1,0:T(8,128)(2,1)}, bf16[512,2048]{1,0:T(8,128)(2,1)S(1)}, u32[]{:S(2)}) copy-start(bf16[512,2048]{1,0:T(8,128)(2,1)S(1)} %fusion.6) | copy-start | bytes 6291460
  224.0 6.4 %copy-start.34 = (bf16[512,1024]{1,0:T(8,128)(2,1)}, bf16[512,1024]{1,0:T(8,128)(2,1)S(1)}, u32[]{:S(2)}) copy-start(bf16[512,1024]{1,0:T(8,128)(2,1)S(1)} %collective-permute-done.2) | copy-start | bytes 3145732
  230.3 11.8 %copy-start.39 = (bf16[512,2048]{1,0:T(8,128)(2,1)}, bf16[512,2048]{1,0:T(8,128)(2,1)S(1)}, u32[]{:S(2)}) copy-start(bf16[512,2048]{1,0:T(8,128)(2,1)S(1)} %get-tuple-element.100) | copy-start | bytes 6291460
  230.3 14.8 %copy-start.38 = (bf16[512,2048]{1,0:T(8,128)(2,1)}, bf16[512,2048]{1,0:T(8,128)(2,1)S(1)}, u32[]{:S(2)}) copy-start(bf16[512,2048]{1,0:T(8,128)(2,1)S(1)} %get-tuple-element.101) | copy-start | bytes 6291460
  230.3 7.8 %copy-start.33 = (bf16[512,1024]{1,0:T(8,128)(2,1)}, bf16[512,1024]{1,0:T(8,128)(2,1)S(1)}, u32[]{:S(2)}) copy-start(bf16[512,1024]{1,0:T(8,128)(2,1)S(1)} %collective-permute-done.4) | copy-start | bytes 3145732
  238.1 2.4 copy-start.16
  240.6 26.2 %collective-permute-start.5 = (bf16[512,1024]{1,0:T(8,128)(2,1)S(1)}, bf16[512,1024]{1,0:T(8,128)(2,1)S(1)}, u32[]{:S(2)}, u32[]{:S(2)}) collective-permute-start(bf16[512,1024]{1,0:T(8,128)(2,1)S(1)} %fusion.87), channel_id=1, source_target_pairs={{0,1},{1,0},{2,3},{3,2},{4,5},{5,4},{6,7},{7,6},{8,9},{9,8},{10,11... | collective-permute-start | bytes 3145736 | tf_op jit(solution)/shard_map/ppermute | solution.py:169
  244.5 43.2 %collective-permute-start.3 = (bf16[512,1024]{1,0:T(8,128)(2,1)S(1)}, bf16[512,1024]{1,0:T(8,128)(2,1)S(1)}, u32[]{:S(2)}, u32[]{:S(2)}) collective-permute-start(bf16[512,1024]{1,0:T(8,128)(2,1)S(1)} %fusion.90), channel_id=1, source_target_pairs={{0,1},{1,0},{2,3},{3,2},{4,5},{5,4},{6,7},{7,6},{8,9},{9,8},{10,11... | collective-permute-start | bytes 3145736 | tf_op jit(solution)/shard_map/ppermute | solution.py:169
  291.0 23.6 %collective-permute-start.6 = (bf16[512,1024]{1,0:T(8,128)(2,1)S(1)}, bf16[512,1024]{1,0:T(8,128)(2,1)S(1)}, u32[]{:S(2)}, u32[]{:S(2)}) collective-permute-start(bf16[512,1024]{1,0:T(8,128)(2,1)S(1)} %get-tuple-element.82), channel_id=1, source_target_pairs={{0,1},{1,0},{2,3},{3,2},{4,5},{5,4},{6,7},{7,6},{8,9},{9,8},{10,11... | collective-permute-start | bytes 3145736 | tf_op jit(solution)/shard_map/ppermute | solution.py:169
  355.3 1.7 copy-start
  355.3 2.0 copy-start.20
  364.9 1.2 copy-start.22
  365.0 10.5 %copy-start.15 = (bf16[512,2048]{1,0:T(8,128)(2,1)S(1)}, bf16[512,2048]{1,0:T(8,128)(2,1)}, u32[]{:S(2)}) copy-start(bf16[512,2048]{1,0:T(8,128)(2,1)} %copy-done.14) | copy-start | bytes 6291460
  365.0 178.9 %reduce-scatter.5.cloned.1.call-start = ((), (), s32[]{:S(2)}) async-start(), calls=%async_computation.7 | async-start | bytes 8912896 | tf_op jit(solution)/shard_map/reduce_scatter | solution.py:303
  366.2 9.3 %copy-start.17 = (bf16[512,2048]{1,0:T(8,128)(2,1)S(1)}, bf16[512,2048]{1,0:T(8,128)(2,1)}, u32[]{:S(2)}) copy-start(bf16[512,2048]{1,0:T(8,128)(2,1)} %copy-done.16) | copy-start | bytes 6291460
  366.2 9.3 %copy-start.24 = (bf16[512,1024]{1,0:T(8,128)(2,1)S(1)}, bf16[512,1024]{1,0:T(8,128)(2,1)}, u32[]{:S(2)}) copy-start(bf16[512,1024]{1,0:T(8,128)(2,1)} %copy-done.23) | copy-start | bytes 3145732
  366.2 9.3 %copy-start.35 = (bf16[512,1024]{1,0:T(8,128)(2,1)S(1)}, bf16[512,1024]{1,0:T(8,128)(2,1)}, u32[]{:S(2)}) copy-start(bf16[512,1024]{1,0:T(8,128)(2,1)} %copy-done.34) | copy-start | bytes 3145732
  390.0 1.9 copy-start.1
  397.1 22.6 %collective-permute-start.7 = (bf16[512,1024]{1,0:T(8,128)(2,1)}, bf16[512,1024]{1,0:T(8,128)(2,1)}, u32[]{:S(2)}, u32[]{:S(2)}) collective-permute-start(bf16[512,1024]{1,0:T(8,128)(2,1)} %fusion.81), channel_id=1, source_target_pairs={{0,1},{1,0},{2,3},{3,2},{4,5},{5,4},{6,7},{7,6},{8,9},{9,8},{10,11... | collective-permute-start | bytes 3145736 | tf_op jit(solution)/shard_map/ppermute | solution.py:169
  401.9 22.9 %copy-start.6 = (bf16[1,512,1024]{2,1,0:T(8,128)(2,1)S(1)}, bf16[1,512,1024]{2,1,0:T(8,128)(2,1)}, u32[]{:S(2)}) copy-start(bf16[1,512,1024]{2,1,0:T(8,128)(2,1)} %param.12) | copy-start | bytes 3145732
  401.9 22.9 %copy-start.7 = (f32[512,1024]{1,0:T(8,128)S(1)}, f32[512,1024]{1,0:T(8,128)}, u32[]{:S(2)}) copy-start(f32[512,1024]{1,0:T(8,128)} %get-tuple-element.102) | copy-start | bytes 6291460
  401.9 22.9 %copy-start.8 = (f32[512,1024]{1,0:T(8,128)S(1)}, f32[512,1024]{1,0:T(8,128)}, u32[]{:S(2)}) copy-start(f32[512,1024]{1,0:T(8,128)} %get-tuple-element.83) | copy-start | bytes 6291460
  402.0 22.9 %copy-start.10 = (bf16[512,1024]{1,0:T(8,128)(2,1)S(1)}, bf16[512,1024]{1,0:T(8,128)(2,1)}, u32[]{:S(2)}) copy-start(bf16[512,1024]{1,0:T(8,128)(2,1)} %copy-done.9) | copy-start | bytes 3145732
  424.9 26.1 %copy-start.13 = (bf16[6,8,8,512]{3,2,0,1:T(8,128)(2,1)S(1)}, bf16[6,8,8,512]{3,2,0,1:T(8,128)(2,1)}, u32[]{:S(2)}) copy-start(bf16[6,8,8,512]{3,2,0,1:T(8,128)(2,1)} %copy-done.12) | copy-start | bytes 1179652
  427.0 34.9 %copy-start.29 = (f32[1,1024]{1,0:T(1,128)S(1)}, f32[1,1024]{1,0:T(1,128)}, u32[]{:S(2)}) copy-start(f32[1,1024]{1,0:T(1,128)} %get-tuple-element.78) | copy-start | bytes 12292
  427.0 3.8 collective-permute-start.8
  452.0 9.7 %all-to-all-start.1 = ((f32[32,1,64]{2,1,0:T(1,128)}), f32[32,1,64]{2,1,0:T(1,128)S(1)}, u32[]{:S(2)}, u32[]{:S(2)}) async-start(f32[32,1,64]{2,1,0:T(1,128)} %bitcast.38), calls=%async_computation.1 | async-start | bytes 32768 | tf_op jit(solution)/shard_map/all_to_all | solution.py:199
  462.4 2.3 copy-start.18
Sparse Core Ops, SparseCore 0:
  10.9 56.8 all-gather.4
  70.7 80.6 all-gather.6
  365.1 70.7 reduce-scatter.2
  440.3 103.4 reduce-scatter.4

commit v2 on v1

--- a/solution.py
+++ b/solution.py
@@ -249,14 +249,15 @@
     row_offset = bias_rows(small_out[4], 2)
     act_rows = lax.dynamic_slice_in_dim(small_out[0], my_dp * rows, rows, axis=1)
 
-    qkv_matrix = lax.all_gather(by_pairs(query_key_value_weight), "dp", axis=0, tiled=True)
-    packed = jnp.concatenate(
-        [attention_output_weight.T, up_projection_weight, down_projection_weight.T], axis=1
-    )
-    packed_full = lax.all_gather(packed, "dp", axis=0, tiled=True)
-    out_matrix_t = packed_full[:, :width]
-    up_matrix = packed_full[:, width : width + ff]
-    down_matrix_t = packed_full[:, width + ff :]
+    packed = jnp.concatenate([by_pairs(query_key_value_weight), attention_output_weight.T], axis=1)
+    attn_full = lax.all_gather(packed, "dp", axis=0, tiled=True)
+    qkv_matrix = attn_full[:, : 3 * width]
+    out_matrix_t = attn_full[:, 3 * width :]
+    packed = jnp.concatenate([up_projection_weight, down_projection_weight.T], axis=1)
+    packed, attn_full = lax.optimization_barrier((packed, attn_full))
+    mlp_full = lax.all_gather(packed, "dp", axis=0, tiled=True)
+    up_matrix = mlp_full[:, :ff]
+    down_matrix_t = mlp_full[:, ff:]
 
     mod_flat = modulation_weight.reshape(rows, -1)
     mod_partial = nn(act_rows, mod_flat)
@@ -275,9 +276,11 @@
     qkv_shift = by_pairs(jnp.stack([qv_offset[0], jnp.zeros_like(qv_offset[0]), qv_offset[1]])[None])
     qkv = joined([(nn(chunk, qkv_matrix) + qkv_shift).astype(bf16) for chunk in chunks_a])
     grad_branch_mlp = (gate_mlp * grad_out).astype(bf16)
+    grad_branch_mlp, qkv = lax.optimization_barrier((grad_branch_mlp, qkv))
     chunks_grad_mlp = expand(grad_branch_mlp)
 
     attended = attend(qkv)
+    attended, chunks_grad_mlp = lax.optimization_barrier((attended, chunks_grad_mlp))
     branch_attn = (
         owned_sums(lambda chunk: nt(chunk, out_matrix_t), chunked(attended, count)) + vectors[6]
     )
@@ -293,16 +296,11 @@
         unused_gelu, gelu_back = jax.vjp(gelu_tanh, pre_chunk)
         grad_pre_up.append(gelu_back(nn(grad_chunk, down_matrix_t))[0].astype(bf16))
     grad_input_m = owned_sums(lambda chunk: nt(chunk, up_matrix), grad_pre_up)
-    branch_mlp = owned_sums(lambda chunk: nt(chunk, down_matrix_t), hidden) + vectors[7]
-    result_out = middle + gate_mlp * branch_mlp
-    grad_gate_mlp = jnp.sum(grad_out * branch_mlp, axis=0)
     grad_pre_full = joined(grad_pre_up)
     up_grad = tn(joined(chunks_m), grad_pre_full).astype(bf16)
     down_grad_t = tn(joined(chunks_grad_mlp), joined(hidden)).astype(bf16)
     up_bias_part = jnp.sum(grad_pre_full, axis=0, dtype=f32)
-    mlp_grads = lax.psum_scatter(
-        jnp.concatenate([up_grad, down_grad_t], axis=1), "dp", scatter_dimension=0, tiled=True
-    ).astype(f32)
+    mlp_packed = jnp.concatenate([up_grad, down_grad_t], axis=1)
 
     grad_shift_mlp = jnp.sum(grad_input_m, axis=0)
     grad_scale_mlp = jnp.sum(grad_input_m * normed_m, axis=0)
@@ -311,13 +309,21 @@
     grad_branch_attn = (gate_attn * grad_middle).astype(bf16)
     chunks_grad_attn = expand(grad_branch_attn)
     grad_attended = joined([nn(chunk, out_matrix_t).astype(bf16) for chunk in chunks_grad_attn])
+    grad_attended, mlp_packed, hidden = lax.optimization_barrier(
+        (grad_attended, mlp_packed, hidden)
+    )
+    mlp_grads = lax.psum_scatter(mlp_packed, "dp", scatter_dimension=0, tiled=True)
+    branch_mlp = owned_sums(lambda chunk: nt(chunk, down_matrix_t), hidden) + vectors[7]
+    result_out = middle + gate_mlp * branch_mlp
+    grad_gate_mlp = jnp.sum(grad_out * branch_mlp, axis=0)
     grad_qkv = attend_back(qkv, grad_attended)
+    grad_qkv, mlp_grads = lax.optimization_barrier((grad_qkv, mlp_grads))
     out_grad_t = tn(joined(chunks_grad_attn), attended).astype(bf16)
     grad_input_a = owned_sums(lambda chunk: nt(chunk, qkv_matrix), chunked(grad_qkv, count))
     qkv_grad = tn(joined(chunks_a), grad_qkv).astype(bf16)
-    attn_grads = lax.psum_scatter(
-        jnp.concatenate([qkv_grad, out_grad_t], axis=1), "dp", scatter_dimension=0, tiled=True
-    ).astype(f32)
+    attn_packed = jnp.concatenate([qkv_grad, out_grad_t], axis=1)
+    attn_grads = lax.psum_scatter(attn_packed, "dp", scatter_dimension=0, tiled=True).astype(f32)
+    mlp_grads = mlp_grads.astype(f32)
     qkv_bias_part = from_pairs(jnp.sum(grad_qkv, axis=0, dtype=f32)[None])[0]
     grad_shift_attn = jnp.sum(grad_input_a, axis=0)
     grad_scale_attn = jnp.sum(grad_input_a * normed_a, axis=0)

time: 561 us -> 498 us (0.89)
  waiting for transfers between devices: 285 us -> 212 us
  matrix products: 80.1 us -> 88.8 us
    ppermute x9, waiting for transfers between devices: 153 us -> 83.9 us  [swap(): return lax.ppermute(values, 'mp', [(0, 1), (1, 0)])]
    all_gather x2, waiting for transfers between devices: 25.5 us -> 51.9 us  [the longest x1 51.9 us: local(): attn_full = lax.all_gather(packed, 'dp', axis=0, tiled=True)]
    reduce_scatter x2, waiting for transfers between devices: 78.4 us -> 52.2 us  [the longest x1 52.2 us: local(): lax.psum_scatter(mlp_packed, 'dp', scatter_dimension=0, tiled=True)]
    dot_general x21, matrix products: 78.4 us -> 87.2 us  [dot(): lax.dot_general(a, b, (contract, ((), ())), preferred_element_type=f32)]
    concatenate x3 -> x4, other arithmetic: 12.4 us -> 13.8 us  [the longest x1 7.79 us: local(): mlp_packed = jnp.concatenate([up_grad, down_grad_t], axis=1)]
  transfers between devices with their start and end apart: 15 -> 15, of which waited for: 12 -> 11; matrix products, arithmetic and copies ran while one was open for 16% -> 21% of each run, Pallas kernels for 5% -> 14%
where the time goes in v2:
time: 498 us; the launch traced here: 491 us
  waiting for transfers between devices  212 us (43%)
  matrix products  88.8 us (18%)
  Pallas kernels  67.1 us (13%)
  blocking collectives  41.8 us (8%)
  other arithmetic  31 us (6%)
  starting transfers between devices  18.3 us (4%)
  local copies, waits for them, and re-layouts  17 us (3%)
  between operations  15 us (3%)
    dot_general x21, matrix products, dot(): lax.dot_general(a, b, (contract, ((), ())), preferred_element_type=f32)  87.2 us
    ppermute x9, waiting for transfers between devices, swap(): return lax.ppermute(values, 'mp', [(0, 1), (1, 0)])  83.9 us
    reduce_scatter x1, waiting for transfers between devices, local(): lax.psum_scatter(mlp_packed, 'dp', scatter_dimension=0, tiled=True)  52.2 us
    all_gather x1, waiting for transfers between devices, local(): attn_full = lax.all_gather(packed, 'dp', axis=0, tiled=True)  51.9 us
    pallas_call x1, Pallas kernels, attend_back(): pl.pallas_call(body, grid=(pairs,), in_specs=[pl.BlockSpec((tokens, 3 * P...  40.1 us
    pallas_call x1, Pallas kernels, attend(): pl.pallas_call(body, grid=(pairs,), in_specs=[pl.BlockSpec((tokens, 3 * P...  27 us
    all_to_all x2, waiting for transfers between devices, to_latents(): received = lax.all_to_all(repeated, ('dp', 'mp'), 0, 0, tiled=True)  24.2 us
    all_gather x1, blocking collectives, local(): everyone = lax.all_gather(mine, 'dp', axis=0, tiled=True)  22.3 us
  transfers between devices with their start and end apart: 15, of which 11 were waited for; matrix products, arithmetic and copies ran while one was open for 21% of the time, Pallas kernels for 14%

profile of v2, /device:TPU:0, one launch (start us, length us, event | category | flops | bytes accessed | tf_op | source)
XLA Modules:
  0.0 491.3 jit_solution(6507682549154999967)
XLA Ops:
  7.3 1.0 reshape.237
  8.7 1.6 pad_maximum_fusion.7
  10.3 1.9 pad_maximum_fusion.6
  12.2 51.9 %all-gather.5.cloned.1.call-done = bf16[1024,2048]{1,0:T(8,128)(2,1)} async-done(((bf16[64,2048]{1,0:T(8,128)(2,1)}), bf16[1024,2048]{1,0:T(8,128)(2,1)}) %all-gather.5.cloned.1.call-update) | async-done | bytes 4194320 | tf_op jit(solution)/shard_map/all_gather | solution.py:253
  65.1 19.5 %all-gather = bf16[16,1,1472]{2,1,0:T(2,128)(2,1)S(1)} all-gather(bf16[1,1,1472]{2,1,0:T(2,128)(2,1)S(1)} %bitcast.176), channel_id=1, replica_groups=mesh['dp'=16,'mp'=2] {'dp'}, dimensions={0}, use_global_device_ids=true | all-gather | bytes 50048 | tf_op jit(solution)/shard_map/all_gather | solution.py:239
  85.7 1.6 all_to_all.12
  87.3 2.6 all-to-all-start
  90.7 21.2 %all-to-all-done = f32[32,1,4096]{2,1,0:T(1,128)S(1)} async-done(((f32[32,1,4096]{2,1,0:T(1,128)}), f32[32,1,4096]{2,1,0:T(1,128)S(1)}, u32[]{:S(2)}, u32[]{:S(2)}) %all-to-all-start) | async-done | bytes 524320 | tf_op jit(solution)/shard_map/all_to_all | solution.py:199
  111.9 1.2 reduce.2
  114.1 1.6 collective-permute-start
  116.3 4.1 fusion.21
  120.4 18.7 %collective-permute-done = bf16[512,1024]{1,0:T(8,128)(2,1)} collective-permute-done((bf16[512,1024]{1,0:T(8,128)(2,1)S(1)}, bf16[512,1024]{1,0:T(8,128)(2,1)}, u32[]{:S(2)}, u32[]{:S(2)}) %collective-permute-start) | collective-permute-done | bytes 1048608 | tf_op jit(solution)/shard_map/ppermute | solution.py:169
  139.1 3.1 fusion.22
  142.8 27.0 %attend.1 = bf16[1024,512]{1,0:T(8,128)(2,1)S(1)} custom-call(bf16[1024,1536]{1,0:T(8,128)(2,1)S(1)} %pad_maximum_fusion.3.qkv_ref.refs_0_), custom_call_target="tpu_custom_call" | custom-call | flops 8589934592 | bytes 4194304 | tf_op jit(solution)/shard_map/attend/pallas_call | solution.py:109
  170.6 1.9 collective-permute-start.2
  172.5 21.8 %collective-permute-done.2 = bf16[512,1024]{1,0:T(8,128)(2,1)S(1)} collective-permute-done((bf16[512,1024]{1,0:T(8,128)(2,1)S(1)}, bf16[512,1024]{1,0:T(8,128)(2,1)S(1)}, u32[]{:S(2)}, u32[]{:S(2)}) %collective-permute-start.2) | collective-permute-done | bytes 1048608 | tf_op jit(solution)/shard_map/ppermute | solution.py:169
  194.3 2.4 fusion.127
  197.0 1.0 copy-done.5
  198.4 1.0 copy-done.25
  199.4 1.7 collective-permute-start.3
  201.1 21.1 %collective-permute-done.3 = bf16[512,1024]{1,0:T(8,128)(2,1)} collective-permute-done((bf16[512,1024]{1,0:T(8,128)(2,1)S(1)}, bf16[512,1024]{1,0:T(8,128)(2,1)}, u32[]{:S(2)}, u32[]{:S(2)}) %collective-permute-start.3) | collective-permute-done | bytes 1048608 | tf_op jit(solution)/shard_map/ppermute | solution.py:169
  222.2 5.0 %fusion.25 = f32[512,2048]{1,0:T(8,128)S(1)} fusion(bf16[512,1024]{1,0:T(8,128)(2,1)} %collective-permute-done.3, bf16[1024,4096]{1,0:T(8,128)(2,1)} %all-gather.7.cloned.1.call-done), kind=kOutput, calls=%fused_computation.42 | convolution fusion | flops 2147483648 | bytes 9437184 | tf_op jit(solution)/shard_map/dot_general | solution.py:35
  227.4 5.2 %fusion.13 = bf16[512,2048]{1,0:T(8,128)(2,1)S(1)} fusion(f32[512,2048]{1,0:T(8,128)S(1)} %fusion.25, f32[2048]{0:T(1024)S(1)} %fusion.113, bf16[512,1024]{1,0:T(8,128)(2,1)S(1)} %copy-done.37, bf16[1024,4096]{1,0:T(8,128)(2,1)S(1)} %copy-done.35), kind=kOutput, calls=%fused_computation.20 | convolution fusion | flops 2169503744 | bytes 11542528 | tf_op jit(solution)/shard_map/dot_general | solution.py:35
  232.6 2.4 fusion.98
  235.0 1.6 collective-permute-start.4
  236.6 5.2 %multiply_convert_fusion.1 = (bf16[512,2048]{1,0:T(8,128)(2,1)S(1)}, bf16[512,2048]{1,0:T(8,128)(2,1)S(1)}, f32[512,2048]{1,0:T(8,128)S(1)}) fusion(f32[2048]{0:T(1024)S(1)} %fusion.113, f32[512,2048]{1,0:T(8,128)S(1)} %fusion.25, bf16[512,1024]{1,0:T(8,128)(2,1)S(1)} %copy-done.26, bf16[1024,4096]{1,0:T(8,128)(2,1)S(1)} %copy-done.35), kind=kOutput, calls=%fused_computation.28 | convolution fusion | flops 2168455168 | bytes 17833984 | tf_op jit(solution)/shard_map/dot_general | solution.py:35
  241.8 6.3 %fusion.18 = bf16[1024,2048]{1,0:T(8,128)(2,1)} fusion(bf16[512,2048]{1,0:T(8,128)(2,1)S(1)} %get-tuple-element.31, bf16[512,2048]{1,0:T(8,128)(2,1)S(1)} %get-tuple-element.30, bf16[512,1024]{1,0:T(8,128)(2,1)S(1)} %copy-done.37, bf16[512,1024]{1,0:T(8,128)(2,1)S(1)} %copy-done.17), kind=kOutput, calls=%fused_computation.29 | convolution fusion | flops 4309647360 | bytes 10485760 | tf_op jit(solution)/shard_map/dot_general | solution.py:35
  248.1 4.8 fusion.6
  252.9 3.9 collective-permute-done.4
  256.8 3.1 multiply_reduce_fusion
  259.9 2.7 convert_reduce_fusion.4
  262.7 1.5 collective-permute-start.5
  264.1 7.6 %convolution_convert_fusion.1 = bf16[1024,2048]{1,0:T(8,128)(2,1)} fusion(bf16[512,2048]{1,0:T(8,128)(2,1)S(1)} %fusion.13, bf16[512,2048]{1,0:T(8,128)(2,1)S(1)} %fusion.6, bf16[512,1024]{1,0:T(8,128)(2,1)} %collective-permute-done.3, bf16[512,1024]{1,0:T(8,128)(2,1)S(1)} %copy-done.26), kind=kOutput, calls=%fused_computation.31 | convolution fusion | flops 4309647360 | bytes 10485760 | tf_op jit(solution)/shard_map/dot_general | solution.py:35
  271.8 7.8 %pad_maximum_fusion = bf16[1024,4096]{1,0:T(8,128)(2,1)} fusion(bf16[1024,2048]{1,0:T(8,128)(2,1)} %fusion.18, bf16[1024,2048]{1,0:T(8,128)(2,1)} %convolution_convert_fusion.1), kind=kLoop, calls=%fused_computation | loop fusion | flops 16777216 | bytes 16777216 | tf_op jit(solution)/shard_map/concatenate | solution.py:303
  279.6 2.2 convolution_convert_fusion.4
  281.8 2.0 collective-permute-done.5
  283.9 2.2 convolution_convert_fusion.3
  286.1 1.1 pad_maximum_fusion.5.refs_1_
  287.3 6.2 %fusion.95 = bf16[512,1024]{1,0:T(8,128)(2,1)} fusion(bf16[512,2048]{1,0:T(8,128)(2,1)} %copy-done.42, bf16[1024,4096]{1,0:T(8,128)(2,1)} %all-gather.7.cloned.1.call-done), kind=kOutput, calls=%fused_computation.117 | convolution fusion | flops 2148007936 | bytes 7340032 | tf_op jit(solution)/shard_map/dot_general | solution.py:35
  293.5 1.3 collective-permute-start.6
  294.9 4.1 fusion.92
  299.0 40.1 %attend_back.1 = bf16[1024,1536]{1,0:T(8,128)(2,1)S(1)} custom-call(bf16[1024,1536]{1,0:T(8,128)(2,1)S(1)} %pad_maximum_fusion.3.qkv_ref.refs_0_, bf16[1024,512]{1,0:T(8,128)(2,1)S(1)} %copy-done.2), custom_call_target="tpu_custom_call" | custom-call | flops 21474836480 | bytes 7340032 | tf_op jit(solution)/shard_map/attend_back/pallas_call | solution.py:133
  339.1 1.7 copy-done
  340.8 52.2 %reduce-scatter.3.cloned.1.call-done = bf16[64,4096]{1,0:T(8,128)(2,1)} async-done(((bf16[1024,4096]{1,0:T(8,128)(2,1)}), bf16[64,4096]{1,0:T(8,128)(2,1)}) %reduce-scatter.3.cloned.1.call-update) | async-done | bytes 524304 | tf_op jit(solution)/shard_map/reduce_scatter | solution.py:315
  393.0 6.0 %convolution_convert_fusion = bf16[1024,1536]{1,0:T(8,128)(2,1)S(1)} fusion(bf16[1024,1536]{1,0:T(8,128)(2,1)} %copy-done, bf16[512,1024]{1,0:T(8,128)(2,1)} %collective-permute-done, bf16[512,1024]{1,0:T(8,128)(2,1)} %copy-done.24), kind=kOutput, calls=%fused_computation.30 | convolution fusion | flops 3226992640 | bytes 8388608 | tf_op jit(solution)/shard_map/dot_general | solution.py:35
  399.0 2.6 pad_maximum_fusion.2
  401.6 1.6 convert_reduce_fusion.3
  403.2 2.9 convert_reduce_fusion
  406.0 4.9 fusion.87
  410.9 1.6 collective-permute-start.7
  412.5 6.5 %fusion.57 = (f32[1024]{0:T(1024)S(1)}, bf16[1,512,1024]{2,1,0:T(8,128)(2,1)}) fusion(bf16[512,1024]{1,0:T(8,128)(2,1)} %collective-permute-done.6, bf16[1,512,1024]{2,1,0:T(8,128)(2,1)S(1)} %copy-done.15, f32[1024]{0:T(1024)S(1)} %bitcast.186, f32[512,1024]{1,0:T(8,128)S(1)} %copy-done.7, f32[1024]{0:T(1024)S(1)} %bitcast.180, ...), kind=kOutput, calls=%fused_computation.76 | convolution fusion | flops 2152201216 | bytes 11546624 | tf_op jit(solution)/shard_map/dot_general | solution.py:35
  419.5 1.1 convert_element_type.219
  421.5 14.8 %collective-permute-done.7 = bf16[512,1024]{1,0:T(8,128)(2,1)} collective-permute-done((bf16[512,1024]{1,0:T(8,128)(2,1)}, bf16[512,1024]{1,0:T(8,128)(2,1)}, u32[]{:S(2)}, u32[]{:S(2)}) %collective-permute-start.7) | collective-permute-done | bytes 1048608 | tf_op jit(solution)/shard_map/ppermute | solution.py:169
  436.3 4.9 %fusion.54 = (f32[1024]{0:T(1024)S(1)}, f32[512]{0:T(512)S(1)}, f32[512]{0:T(512)S(1)}, f32[1024]{0:T(1024)S(1)}, f32[512,1024]{1,0:T(8,128)S(1)}) fusion(bf16[1,512,1024]{2,1,0:T(8,128)(2,1)} %param.12, f32[512]{0:T(512)S(1)} %add_rsqrt_fusion.1, f32[512]{0:T(512)S(1)} %broadcast_multiply_fusion.5, f32[1024]{0:T(1024)S(1)} %bitcast.169, ...), kind=kOutput, calls=%fused_computation.73 | convolution fusion | flops 1616901120 | bytes 8933376 | tf_op jit(solution)/shard_map/dot_general | solution.py:35
  441.3 1.9 multiply_reduce_fusion.1
  443.3 1.5 collective-permute-start.8
  445.6 1.4 collective-permute-done.8
  447.1 22.3 %all-gather.1 = f32[16,1,7168]{2,1,0:T(1,128)S(1)} all-gather(f32[1,1,7168]{2,1,0:T(1,128)S(1)} %maximum_bitcast_fusion), channel_id=1, replica_groups=mesh['dp'=16,'mp'=2] {'dp'}, dimensions={0}, use_global_device_ids=true | all-gather | bytes 487424 | tf_op jit(solution)/shard_map/all_gather | solution.py:354
  470.9 2.5 all-to-all-start.1
  474.1 1.3 fusion.109
  476.1 0.9 copy.61
  477.6 3.0 all-to-all-done.1
  481.3 1.0 slice.182
  482.7 0.9 reshape.244
  (173 shorter events, 14.6 us)
Async XLA Ops:
  7.2 57.0 %copy-start.38 = (bf16[2,32]{1,0:T(2,128)(2,1)S(1)}, bf16[2,32]{1,0:T(2,128)(2,1)}, u32[]{:S(2)}) copy-start(bf16[2,32]{1,0:T(2,128)(2,1)} %param.17) | copy-start | bytes 388
  7.2 57.0 %copy-start.39 = (bf16[2,32]{1,0:T(2,128)(2,1)S(1)}, bf16[2,32]{1,0:T(2,128)(2,1)}, u32[]{:S(2)}) copy-start(bf16[2,32]{1,0:T(2,128)(2,1)} %param.22) | copy-start | bytes 388
  7.2 57.1 %copy-start.33 = (bf16[6,32]{1,0:T(8,128)(2,1)S(1)}, bf16[6,32]{1,0:T(8,128)(2,1)}, u32[]{:S(2)}) copy-start(bf16[6,32]{1,0:T(8,128)(2,1)} %param.15) | copy-start | bytes 1156
  7.2 57.2 %copy-start.31 = (bf16[1,1024]{1,0:T(2,128)(2,1)S(1)}, bf16[1,1024]{1,0:T(2,128)(2,1)}, u32[]{:S(2)}) copy-start(bf16[1,1024]{1,0:T(2,128)(2,1)} %param.13) | copy-start | bytes 6148
  7.2 57.8 %copy-start.34 = (bf16[128]{0:T(256)(128)(2,1)S(1)}, bf16[128]{0:T(256)(128)(2,1)}, u32[]{:S(2)}) copy-start(bf16[128]{0:T(256)(128)(2,1)} %param.20) | copy-start | bytes 772
  7.2 77.8 %copy-start.28 = (bf16[64,6,512]{2,0,1:T(8,128)(2,1)S(1)}, bf16[64,6,512]{2,0,1:T(8,128)(2,1)}, u32[]{:S(2)}) copy-start(bf16[64,6,512]{2,0,1:T(8,128)(2,1)} %param.14) | copy-start | bytes 1179652
  7.2 56.9 %all-gather.5.cloned.1.call-start = ((), (), s32[]{:S(2)}) async-start(), calls=%async_computation.4 | async-start | bytes 4456448 | tf_op jit(solution)/shard_map/all_gather | solution.py:253
  10.3 211.9 %all-gather.7.cloned.1.call-start = ((), (), s32[]{:S(2)}) async-start(), calls=%async_computation.5 | async-start | bytes 8912896 | tf_op jit(solution)/shard_map/all_gather | solution.py:258
  12.2 77.9 %copy-start.8 = (bf16[1,512,1024]{2,1,0:T(8,128)(2,1)S(1)}, bf16[1,512,1024]{2,1,0:T(8,128)(2,1)}, u32[]{:S(2)}) copy-start(bf16[1,512,1024]{2,1,0:T(8,128)(2,1)} %param.12) | copy-start | bytes 3145732
  84.6 0.8 copy-start.30
  85.1 4.9 %copy-start.18 = (bf16[6,8,8,512]{3,2,0,1:T(8,128)(2,1)}, bf16[6,8,8,512]{3,2,0,1:T(8,128)(2,1)S(1)}, u32[]{:S(2)}) copy-start(bf16[6,8,8,512]{3,2,0,1:T(8,128)(2,1)S(1)} %copy.52) | copy-start | bytes 1179652
  87.3 24.6 %all-to-all-start = ((f32[32,1,4096]{2,1,0:T(1,128)}), f32[32,1,4096]{2,1,0:T(1,128)S(1)}, u32[]{:S(2)}, u32[]{:S(2)}) async-start(f32[32,1,4096]{2,1,0:T(1,128)} %all_to_all.12), calls=%async_computation | async-start | bytes 1048576 | tf_op jit(solution)/shard_map/all_to_all | solution.py:199
  89.9 303.0 %reduce-scatter.3.cloned.1.call-start = ((), (), s32[]{:S(2)}) async-start(), calls=%async_computation.6 | async-start | bytes 8912896 | tf_op jit(solution)/shard_map/reduce_scatter | solution.py:315
  90.3 25.8 %copy-start.13 = (bf16[1,512,1024]{2,1,0:T(8,128)(2,1)S(1)}, bf16[1,512,1024]{2,1,0:T(8,128)(2,1)}, u32[]{:S(2)}) copy-start(bf16[1,512,1024]{2,1,0:T(8,128)(2,1)} %param.23) | copy-start | bytes 3145732
  114.1 6.3 %copy-start.24 = (bf16[512,1024]{1,0:T(8,128)(2,1)}, bf16[512,1024]{1,0:T(8,128)(2,1)S(1)}, u32[]{:S(2)}) copy-start(bf16[512,1024]{1,0:T(8,128)(2,1)S(1)} %fusion.48) | copy-start | bytes 3145732
  114.1 25.0 %collective-permute-start = (bf16[512,1024]{1,0:T(8,128)(2,1)S(1)}, bf16[512,1024]{1,0:T(8,128)(2,1)}, u32[]{:S(2)}, u32[]{:S(2)}) collective-permute-start(bf16[512,1024]{1,0:T(8,128)(2,1)S(1)} %fusion.48), channel_id=1, source_target_pairs={{0,1},{1,0},{2,3},{3,2},{4,5},{5,4},{6,7},{7,6},{8,9},{9,8},{10,11... | collective-permute-start | bytes 3145736 | tf_op jit(solution)/shard_map/ppermute | solution.py:169
  116.3 26.2 %copy-start.16 = (bf16[512,1024]{1,0:T(8,128)(2,1)}, bf16[512,1024]{1,0:T(8,128)(2,1)S(1)}, u32[]{:S(2)}) copy-start(bf16[512,1024]{1,0:T(8,128)(2,1)S(1)} %fusion.56) | copy-start | bytes 3145732
  116.3 22.8 %copy-start.29 = (bf16[1024,2048]{1,0:T(8,128)(2,1)S(1)}, bf16[1024,2048]{1,0:T(8,128)(2,1)}, u32[]{:S(2)}) copy-start(bf16[1024,2048]{1,0:T(8,128)(2,1)} %all-gather.5.cloned.1.call-done) | copy-start | bytes 12582916
  142.5 27.3 %collective-permute-start.1 = (bf16[512,1024]{1,0:T(8,128)(2,1)S(1)}, bf16[512,1024]{1,0:T(8,128)(2,1)S(1)}, u32[]{:S(2)}, u32[]{:S(2)}) collective-permute-start(bf16[512,1024]{1,0:T(8,128)(2,1)S(1)} %fusion.56), channel_id=1, source_target_pairs={{0,1},{1,0},{2,3},{3,2},{4,5},{5,4},{6,7},{7,6},{8,9},{9,8},{10,11... | collective-permute-start | bytes 3145736 | tf_op jit(solution)/shard_map/ppermute | solution.py:169
  169.8 26.9 %copy-start.3 = (bf16[1024,512]{1,0:T(8,128)(2,1)}, bf16[1024,512]{1,0:T(8,128)(2,1)S(1)}, u32[]{:S(2)}) copy-start(bf16[1024,512]{1,0:T(8,128)(2,1)S(1)} %attend.1) | copy-start | bytes 3145732
  169.8 24.5 %copy-start.9 = (bf16[1,512,1024]{2,1,0:T(8,128)(2,1)S(1)}, bf16[1,512,1024]{2,1,0:T(8,128)(2,1)}, u32[]{:S(2)}) copy-start(bf16[1,512,1024]{2,1,0:T(8,128)(2,1)} %param.12) | copy-start | bytes 3145732
  169.8 26.8 %copy-start.36 = (bf16[512,1024]{1,0:T(8,128)(2,1)}, bf16[512,1024]{1,0:T(8,128)(2,1)S(1)}, u32[]{:S(2)}) copy-start(bf16[512,1024]{1,0:T(8,128)(2,1)S(1)} %collective-permute-done.1) | copy-start | bytes 3145732
  170.6 23.7 %collective-permute-start.2 = (bf16[512,1024]{1,0:T(8,128)(2,1)S(1)}, bf16[512,1024]{1,0:T(8,128)(2,1)S(1)}, u32[]{:S(2)}, u32[]{:S(2)}) collective-permute-start(bf16[512,1024]{1,0:T(8,128)(2,1)S(1)} %convolution_convert_fusion.2), channel_id=1, source_target_pairs={{0,1},{1,0},{2,3},{3,2},{4,5},{5,4},{6,7},{7,6},{8,9},{9,8},{10,11... | collective-permute-start | bytes 3145736 | tf_op jit(solution)/shard_map/ppermute | solution.py:169
  196.7 1.3 copy-start.5
  198.4 1.0 copy-start.25
  199.4 22.8 %collective-permute-start.3 = (bf16[512,1024]{1,0:T(8,128)(2,1)S(1)}, bf16[512,1024]{1,0:T(8,128)(2,1)}, u32[]{:S(2)}, u32[]{:S(2)}) collective-permute-start(bf16[512,1024]{1,0:T(8,128)(2,1)S(1)} %add_convert_fusion.1), channel_id=1, source_target_pairs={{0,1},{1,0},{2,3},{3,2},{4,5},{5,4},{6,7},{7,6},{8,9},{9,8},{10,11... | collective-permute-start | bytes 3145736 | tf_op jit(solution)/shard_map/ppermute | solution.py:169
  222.2 5.0 %copy-start.35 = (bf16[1024,4096]{1,0:T(8,128)(2,1)S(1)}, bf16[1024,4096]{1,0:T(8,128)(2,1)}, u32[]{:S(2)}) copy-start(bf16[1024,4096]{1,0:T(8,128)(2,1)} %all-gather.7.cloned.1.call-done) | copy-start | bytes 25165828
  222.2 5.2 %copy-start.37 = (bf16[512,1024]{1,0:T(8,128)(2,1)S(1)}, bf16[512,1024]{1,0:T(8,128)(2,1)}, u32[]{:S(2)}) copy-start(bf16[512,1024]{1,0:T(8,128)(2,1)} %copy-done.36) | copy-start | bytes 3145732
  232.5 31.6 %copy-start.21 = (bf16[512,2048]{1,0:T(8,128)(2,1)}, bf16[512,2048]{1,0:T(8,128)(2,1)S(1)}, u32[]{:S(2)}) copy-start(bf16[512,2048]{1,0:T(8,128)(2,1)S(1)} %fusion.13) | copy-start | bytes 6291460
  232.5 4.1 copy-start.26
  234.9 6.9 %copy-start.17 = (bf16[512,1024]{1,0:T(8,128)(2,1)S(1)}, bf16[512,1024]{1,0:T(8,128)(2,1)}, u32[]{:S(2)}) copy-start(bf16[512,1024]{1,0:T(8,128)(2,1)} %copy-done.16) | copy-start | bytes 3145732
  235.0 21.9 %collective-permute-start.4 = (bf16[512,1024]{1,0:T(8,128)(2,1)S(1)}, bf16[512,1024]{1,0:T(8,128)(2,1)S(1)}, u32[]{:S(2)}, u32[]{:S(2)}) collective-permute-start(bf16[512,1024]{1,0:T(8,128)(2,1)S(1)} %fusion.98), channel_id=1, source_target_pairs={{0,1},{1,0},{2,3},{3,2},{4,5},{5,4},{6,7},{7,6},{8,9},{9,8},{10,11... | collective-permute-start | bytes 3145736 | tf_op jit(solution)/shard_map/ppermute | solution.py:169
  241.8 6.3 %copy-start.40 = (bf16[512,2048]{1,0:T(8,128)(2,1)}, bf16[512,2048]{1,0:T(8,128)(2,1)S(1)}, u32[]{:S(2)}) copy-start(bf16[512,2048]{1,0:T(8,128)(2,1)S(1)} %get-tuple-element.30) | copy-start | bytes 6291460
  241.8 6.3 %copy-start.42 = (bf16[512,2048]{1,0:T(8,128)(2,1)}, bf16[512,2048]{1,0:T(8,128)(2,1)S(1)}, u32[]{:S(2)}) copy-start(bf16[512,2048]{1,0:T(8,128)(2,1)S(1)} %get-tuple-element.31) | copy-start | bytes 6291460
  248.1 8.7 %copy-start.6 = (f32[512,1024]{1,0:T(8,128)S(1)}, f32[512,1024]{1,0:T(8,128)}, u32[]{:S(2)}) copy-start(f32[512,1024]{1,0:T(8,128)} %copy-done.5) | copy-start | bytes 6291460
  252.9 11.3 %copy-start.22 = (bf16[512,2048]{1,0:T(8,128)(2,1)}, bf16[512,2048]{1,0:T(8,128)(2,1)S(1)}, u32[]{:S(2)}) copy-start(bf16[512,2048]{1,0:T(8,128)(2,1)S(1)} %fusion.6) | copy-start | bytes 6291460
  252.9 7.0 %copy-start.14 = (bf16[1,512,1024]{2,1,0:T(8,128)(2,1)S(1)}, bf16[1,512,1024]{2,1,0:T(8,128)(2,1)}, u32[]{:S(2)}) copy-start(bf16[1,512,1024]{2,1,0:T(8,128)(2,1)} %param.23) | copy-start | bytes 3145732
  262.7 21.2 %collective-permute-start.5 = (bf16[512,1024]{1,0:T(8,128)(2,1)}, bf16[512,1024]{1,0:T(8,128)(2,1)}, u32[]{:S(2)}, u32[]{:S(2)}) collective-permute-start(bf16[512,1024]{1,0:T(8,128)(2,1)} %get-tuple-element.95), channel_id=1, source_target_pairs={{0,1},{1,0},{2,3},{3,2},{4,5},{5,4},{6,7},{7,6},{8,9},{9,8},{10,11... | collective-permute-start | bytes 3145736 | tf_op jit(solution)/shard_map/ppermute | solution.py:169
  287.2 194.1 %reduce-scatter.5.cloned.1.call-start = ((), (), s32[]{:S(2)}) async-start(), calls=%async_computation.7 | async-start | bytes 4456448 | tf_op jit(solution)/shard_map/reduce_scatter | solution.py:325
  287.3 7.6 %copy-start.4 = (bf16[1024,512]{1,0:T(8,128)(2,1)S(1)}, bf16[1024,512]{1,0:T(8,128)(2,1)}, u32[]{:S(2)}) copy-start(bf16[1024,512]{1,0:T(8,128)(2,1)} %copy-done.3) | copy-start | bytes 3145732
  293.5 5.5 %copy-start.2 = (bf16[1024,512]{1,0:T(8,128)(2,1)S(1)}, bf16[1024,512]{1,0:T(8,128)(2,1)}, u32[]{:S(2)}) copy-start(bf16[1024,512]{1,0:T(8,128)(2,1)} %pad_maximum_fusion.5.refs_1_) | copy-start | bytes 3145732
  293.5 119.0 %collective-permute-start.6 = (bf16[512,1024]{1,0:T(8,128)(2,1)}, bf16[512,1024]{1,0:T(8,128)(2,1)}, u32[]{:S(2)}, u32[]{:S(2)}) collective-permute-start(bf16[512,1024]{1,0:T(8,128)(2,1)} %fusion.95), channel_id=1, source_target_pairs={{0,1},{1,0},{2,3},{3,2},{4,5},{5,4},{6,7},{7,6},{8,9},{9,8},{10,11... | collective-permute-start | bytes 3145736 | tf_op jit(solution)/shard_map/ppermute | solution.py:169
  339.1 1.7 copy-start
  340.8 58.2 %copy-start.27 = (bf16[1024,512]{1,0:T(8,128)(2,1)S(1)}, bf16[1024,512]{1,0:T(8,128)(2,1)}, u32[]{:S(2)}) copy-start(bf16[1024,512]{1,0:T(8,128)(2,1)} %fusion.92) | copy-start | bytes 3145732
  401.6 4.4 copy-start.1
  406.0 6.5 %copy-start.7 = (f32[512,1024]{1,0:T(8,128)S(1)}, f32[512,1024]{1,0:T(8,128)}, u32[]{:S(2)}) copy-start(f32[512,1024]{1,0:T(8,128)} %copy-done.5) | copy-start | bytes 6291460
  406.0 6.5 %copy-start.15 = (bf16[1,512,1024]{2,1,0:T(8,128)(2,1)S(1)}, bf16[1,512,1024]{2,1,0:T(8,128)(2,1)}, u32[]{:S(2)}) copy-start(bf16[1,512,1024]{2,1,0:T(8,128)(2,1)} %param.23) | copy-start | bytes 3145732
  406.0 6.5 %copy-start.41 = (bf16[512,2048]{1,0:T(8,128)(2,1)S(1)}, bf16[512,2048]{1,0:T(8,128)(2,1)}, u32[]{:S(2)}) copy-start(bf16[512,2048]{1,0:T(8,128)(2,1)} %copy-done.40) | copy-start | bytes 6291460
  410.9 25.4 %collective-permute-start.7 = (bf16[512,1024]{1,0:T(8,128)(2,1)}, bf16[512,1024]{1,0:T(8,128)(2,1)}, u32[]{:S(2)}, u32[]{:S(2)}) collective-permute-start(bf16[512,1024]{1,0:T(8,128)(2,1)} %fusion.87), channel_id=1, source_target_pairs={{0,1},{1,0},{2,3},{3,2},{4,5},{5,4},{6,7},{7,6},{8,9},{9,8},{10,11... | collective-permute-start | bytes 3145736 | tf_op jit(solution)/shard_map/ppermute | solution.py:169
  421.5 19.8 %copy-start.10 = (bf16[1,512,1024]{2,1,0:T(8,128)(2,1)S(1)}, bf16[1,512,1024]{2,1,0:T(8,128)(2,1)}, u32[]{:S(2)}) copy-start(bf16[1,512,1024]{2,1,0:T(8,128)(2,1)} %param.12) | copy-start | bytes 3145732
  421.5 19.8 %copy-start.11 = (f32[512,1024]{1,0:T(8,128)S(1)}, f32[512,1024]{1,0:T(8,128)}, u32[]{:S(2)}) copy-start(f32[512,1024]{1,0:T(8,128)} %get-tuple-element.121) | copy-start | bytes 6291460
  421.5 19.8 %copy-start.12 = (f32[512,1024]{1,0:T(8,128)S(1)}, f32[512,1024]{1,0:T(8,128)}, u32[]{:S(2)}) copy-start(f32[512,1024]{1,0:T(8,128)} %get-tuple-element.96) | copy-start | bytes 6291460
  441.3 3.5 copy-start.20
  443.2 26.7 %copy-start.19 = (bf16[6,8,8,512]{3,2,0,1:T(8,128)(2,1)S(1)}, bf16[6,8,8,512]{3,2,0,1:T(8,128)(2,1)}, u32[]{:S(2)}) copy-start(bf16[6,8,8,512]{3,2,0,1:T(8,128)(2,1)} %copy-done.18) | copy-start | bytes 1179652
  443.3 3.8 collective-permute-start.8
  444.8 35.9 %copy-start.32 = (f32[1,1024]{1,0:T(1,128)S(1)}, f32[1,1024]{1,0:T(1,128)}, u32[]{:S(2)}) copy-start(f32[1,1024]{1,0:T(1,128)} %get-tuple-element.100) | copy-start | bytes 12292
  470.9 9.7 %all-to-all-start.1 = ((f32[32,1,64]{2,1,0:T(1,128)}), f32[32,1,64]{2,1,0:T(1,128)S(1)}, u32[]{:S(2)}, u32[]{:S(2)}) async-start(f32[32,1,64]{2,1,0:T(1,128)} %bitcast.38), calls=%async_computation.2 | async-start | bytes 32768 | tf_op jit(solution)/shard_map/all_to_all | solution.py:199
  481.3 2.3 copy-start.23
Sparse Core Ops, SparseCore 0:
  10.8 53.2 all-gather.4
  66.8 75.5 all-gather.6
  287.3 105.6 reduce-scatter.2
  401.7 73.4 reduce-scatter.4
